TPU v7x, 512 devices: a whole 4x4x16 slice. The times are simulated.
512 devices in a mesh: seq: 64 (over y, z), rep: 8 (over x, core).
Axes of the slice: x: 4, y: 4, z: 16, core: 2. Of those that a mesh axis runs over, the one named last changes fastest.
Arguments:
- q_lin: bfloat16 [8, 8192, 4096], P('rep', 'seq'), may hold values from -90 to 90, as said below
- k_lin: bfloat16 [8, 8192, 512], P('rep', 'seq'), may hold values from -4 to 4
- value_projection: bfloat16 [8, 8192, 512], P('rep', 'seq'), may hold values from -6 to 6
- grad_out: bfloat16 [8, 8192, 4096], P('rep', 'seq'), may hold values from -6 to 6
- q_bias: float32 [4096], replicated, may hold values from -3 to 3
- block_lists: int32 [32, 64, 2], replicated, may hold values from 0 to 63, as said below
- block_counts: int32 [32, 64], replicated, may hold values from 1 to 2, as said below
Outputs:
- dq: bfloat16 [8, 8192, 4096], P('rep', 'seq')
- dk: bfloat16 [8, 8192, 512], P('rep', 'seq')
- dv: bfloat16 [8, 8192, 512], P('rep', 'seq')
- dbq: float32 [4096], replicated
Inputs may be any that keep to these rules, and one draw needn't show every extreme that they name: `q_lin`: in the shown and hidden draws alike the entries stay within the stated range. `block_lists`: entry 0 of every list is the query block itself; the 2 entries of a list are distinct; entries past block_counts are ignored. `block_counts`: some head has 2 for every query block.
All inputs are finite; a program needn't handle non-finite values.
Results may differ from a plain program's by a relative error of at most 0.008.
Values may be sent and summed in bfloat16 or wider, within the bound.
No kernel may reach another device: no remote copies, remote signals or barrier semaphores. Data moves between devices by JAX's collectives and lax.ppermute only.
A program may use at most 128 MiB of HBM per device.

v0:
```python
import functools

import jax
import jax.numpy as jnp
from jax import lax
from jax.sharding import Mesh
from jax.sharding import PartitionSpec as P

SEQ = ("seq_0", "seq_1")
SEQ_REP = ("seq_0", "seq_1", "rep_0", "rep_1")
REP = ("rep_0", "rep_1")


masked_score = -1e30


def in_one_piece(arrays, axis, split_dim, concat_dim, along):
    widths = [a.shape[along] for a in arrays]
    both = jnp.concatenate(arrays, axis=along)
    filled = lax.all_to_all(both, axis, split_axis=split_dim, concat_axis=concat_dim, tiled=True)
    return tuple(jnp.split(filled, [sum(widths[:k]) for k in range(1, len(widths))], axis=along))


def one_axis_at_a_time(x, axes):
    return functools.reduce(lax.psum, axes, x)


def unit_layout(values_in, part_count, slice_rows, head_count, head_dim):
    shaped = values_in.reshape(part_count, slice_rows, head_count, head_dim)
    return jnp.transpose(shaped, (1, 2, 0, 3)).reshape(
        slice_rows, head_count * part_count, head_dim
    )


def tile_pass(query_rows, grads, chosen, counts, key_blocks, value_blocks, scaling):
    tile_count, row_count, head_dim = query_rows.shape
    list_width = chosen.shape[1]
    block_total, block_rows, _ = key_blocks.shape
    key_tiles = jnp.take(key_blocks, chosen, axis=0).reshape(
        tile_count, list_width * block_rows, head_dim
    )
    value_tiles = jnp.take(value_blocks, chosen, axis=0).reshape(
        tile_count, list_width * block_rows, head_dim
    )
    active = jnp.repeat(
        jnp.arange(list_width, dtype=jnp.int32)[None, :] < counts[:, None], block_rows, axis=1
    )
    scores = (
        jnp.einsum("tqd,tkd->tqk", query_rows, key_tiles, preferred_element_type=jnp.float32)
        * scaling
    )
    scores = jnp.where(active[:, None, :], scores, masked_score)
    weights = jax.nn.softmax(scores, axis=-1)
    weights_half = weights.astype(jnp.bfloat16)
    attn_out = jnp.einsum(
        "tqk,tkd->tqd", weights_half, value_tiles, preferred_element_type=jnp.float32
    )
    row_dots = jnp.sum(grads.astype(jnp.float32) * attn_out, axis=2)
    weight_grads = jnp.einsum(
        "tqd,tkd->tqk", grads, value_tiles, preferred_element_type=jnp.float32
    )
    score_grads = (weights * (weight_grads - row_dots[:, :, None])).astype(jnp.bfloat16)
    grad_q = scaling * jnp.einsum(
        "tqk,tkd->tqd", score_grads, key_tiles, preferred_element_type=jnp.float32
    )
    key_update = scaling * jnp.einsum(
        "tqk,tqd->tkd", score_grads, query_rows, preferred_element_type=jnp.float32
    )
    value_update = jnp.einsum(
        "tqk,tqd->tkd", weights_half, grads, preferred_element_type=jnp.float32
    )
    selector = (
        chosen.reshape(tile_count * list_width)[:, None]
        == jnp.arange(block_total, dtype=jnp.int32)[None, :]
    ).astype(jnp.float32)
    key_gradient = jnp.einsum(
        "mn,mrd->nrd",
        selector,
        key_update.reshape(tile_count * list_width, block_rows, head_dim),
        precision=lax.Precision.HIGHEST,
        preferred_element_type=jnp.float32,
    )
    value_gradient = jnp.einsum(
        "mn,mrd->nrd",
        selector,
        value_update.reshape(tile_count * list_width, block_rows, head_dim),
        precision=lax.Precision.HIGHEST,
        preferred_element_type=jnp.float32,
    )
    return (grad_q, key_gradient, value_gradient)


def body(q_lin, k_lin, value_projection, grad_out, q_bias, block_lists, block_counts):
    devices = lax.axis_size(SEQ)
    my_index = lax.axis_index(SEQ)
    tok_rows = q_lin.shape[1]
    head_count, qblock_count, list_width = block_lists.shape
    head_dim = q_bias.shape[0] // head_count
    kv_count = k_lin.shape[2] // head_dim
    part_count = 2 * devices // head_count
    slice_rows = tok_rows // part_count
    block_rows = tok_rows * devices // qblock_count
    tile_rows = min(slice_rows, block_rows)
    per_slice = slice_rows // tile_rows
    tile_count = devices * per_slice
    unit_count = head_count * part_count
    scaling = head_dim ** (-0.5)
    placing = jnp.arange(unit_count, dtype=jnp.int32)
    query_rows = (q_lin[0].astype(jnp.float32) + q_bias).astype(jnp.bfloat16)
    send_q = jnp.take(
        unit_layout(query_rows, part_count, slice_rows, head_count, head_dim), placing, axis=1
    )
    send_g = jnp.take(
        unit_layout(grad_out[0], part_count, slice_rows, head_count, head_dim), placing, axis=1
    )
    send_q = send_q.reshape(slice_rows, devices, 2, head_dim)
    send_g = send_g.reshape(slice_rows, devices, 2, head_dim)
    got_q, got_g = in_one_piece((send_q, send_g), SEQ, 1, 0, 2)
    got_q = got_q.reshape(tile_count, tile_rows, 2, head_dim)
    got_g = got_g.reshape(tile_count, tile_rows, 2, head_dim)
    copies = devices // kv_count
    send_k = jnp.repeat(k_lin[0].reshape(tok_rows, kv_count, head_dim), copies, axis=1)
    send_v = jnp.repeat(value_projection[0].reshape(tok_rows, kv_count, head_dim), copies, axis=1)
    got_k, got_v = in_one_piece((send_k, send_v), SEQ, 1, 0, 2)
    key_blocks = got_k.reshape(qblock_count, block_rows, head_dim)
    value_blocks = got_v.reshape(qblock_count, block_rows, head_dim)
    my_units = lax.dynamic_slice_in_dim(placing, 2 * my_index, 2)
    head_of = my_units // part_count
    part_of = my_units % part_count
    tile_ids = jnp.arange(tile_count, dtype=jnp.int32)
    first_row = (
        tile_ids // per_slice * tok_rows
        + part_of[0] * slice_rows
        + tile_ids % per_slice * tile_rows
    )
    block_ids = first_row // block_rows
    head_lists = lax.dynamic_index_in_dim(block_lists, head_of[0], 0, keepdims=False)
    head_counts = lax.dynamic_index_in_dim(block_counts, head_of[0], 0, keepdims=False)
    chosen = jnp.take(head_lists, block_ids, axis=0)
    counts = jnp.take(head_counts, block_ids, axis=0)
    both_q = jnp.concatenate([got_q[:, :, 0], got_q[:, :, 1]], axis=1)
    both_g = jnp.concatenate([got_g[:, :, 0], got_g[:, :, 1]], axis=1)
    grad_both, key_total, value_total = tile_pass(
        both_q, both_g, chosen, counts, key_blocks, value_blocks, scaling
    )
    unit_grads = [grad_both[:, :tile_rows], grad_both[:, tile_rows:]]
    unit_sums = jnp.stack([jnp.sum(grad_one, axis=(0, 1)) for grad_one in unit_grads])
    unit_selector = (my_units[:, None] == jnp.arange(unit_count, dtype=jnp.int32)[None, :]).astype(
        jnp.float32
    )
    bias_parts = jnp.einsum(
        "mu,md->ud",
        unit_selector,
        unit_sums,
        precision=lax.Precision.HIGHEST,
        preferred_element_type=jnp.float32,
    )
    bias_total = one_axis_at_a_time(bias_parts, SEQ_REP)
    dq_send = jnp.stack(unit_grads, axis=2).astype(jnp.bfloat16)
    back_q = lax.all_to_all(dq_send, SEQ, split_axis=0, concat_axis=0, tiled=True)
    back_k, back_v = tuple(
        (
            part.astype(jnp.float32)
            for part in in_one_piece(
                (key_total.astype(jnp.bfloat16), value_total.astype(jnp.bfloat16)), SEQ, 0, 0, 1
            )
        )
    )
    arrived = jnp.transpose(back_q, (0, 2, 1, 3)).reshape(unit_count, slice_rows, head_dim)
    unit_ids = jnp.arange(unit_count, dtype=jnp.int32)
    inverse = jnp.sum(
        jnp.where(placing[:, None] == unit_ids[None, :], unit_ids[:, None], 0), axis=0
    )
    by_unit = jnp.take(arrived, inverse, axis=0).reshape(
        head_count, part_count, slice_rows, head_dim
    )
    dq_out = jnp.transpose(by_unit, (1, 2, 0, 3)).reshape(1, tok_rows, head_count * head_dim)
    dk_sum = jnp.sum(back_k.reshape(kv_count, copies, tok_rows, head_dim), axis=1)
    dv_sum = jnp.sum(back_v.reshape(kv_count, copies, tok_rows, head_dim), axis=1)
    dk_out = (
        jnp.transpose(dk_sum, (1, 0, 2))
        .reshape(1, tok_rows, kv_count * head_dim)
        .astype(jnp.bfloat16)
    )
    dv_out = (
        jnp.transpose(dv_sum, (1, 0, 2))
        .reshape(1, tok_rows, kv_count * head_dim)
        .astype(jnp.bfloat16)
    )
    bias_out = jnp.sum(bias_total.reshape(head_count, part_count, head_dim), axis=1).reshape(
        head_count * head_dim
    )
    return (dq_out, dk_out, dv_out, bias_out)


def solution(mesh):
    torus = Mesh(mesh.devices.reshape(4, 16, 4, 2), ("seq_0", "seq_1", "rep_0", "rep_1"))
    placed = (
        P(REP, SEQ, None),
        P(REP, SEQ, None),
        P(REP, SEQ, None),
        P(REP, SEQ, None),
        P(),
        P(),
        P(),
    )
    return jax.shard_map(
        body,
        mesh=torus,
        in_specs=placed,
        out_specs=(P(REP, SEQ, None), P(REP, SEQ, None), P(REP, SEQ, None), P()),
        check_vma=False,
    )
```

profile of v0, /device:TPU:1, one launch (start us, length us, event | category | flops | bytes accessed | tf_op | source)
XLA Modules:
  0.0 766.9 jit_solution(10066897023720417863)
XLA Ops:
  7.2 1.5 copy.85
  8.9 0.4 copy.69
  10.2 0.4 copy.68
  10.7 0.8 gather_fusion.4
  11.4 0.8 gather_fusion.3
  12.5 1.5 pad_maximum_fusion.2
  14.0 19.3 %all-to-all-start = ((bf16[32,64,4,128]{3,0,2,1:T(8,128)(2,1)}), bf16[32,64,4,128]{3,0,2,1:T(8,128)(2,1)S(1)}, u32[]{:S(2)}, u32[]{:S(2)}) async-start(bf16[32,64,4,128]{3,0,2,1:T(8,128)(2,1)} %pad_maximum_fusion.2), calls=%async_computation | async-start | bytes 4194304 | tf_op jit(solution)/shard_map/all_to_all | solution.py:20
  33.5 0.5 broadcast_in_dim.96
  34.0 0.5 broadcast_in_dim.95
  34.5 2.7 pad_maximum_fusion
  37.1 91.0 %all-to-all-done = bf16[32,64,4,128]{3,0,2,1:T(8,128)(2,1)S(1)} async-done(((bf16[32,64,4,128]{3,0,2,1:T(8,128)(2,1)}), bf16[32,64,4,128]{3,0,2,1:T(8,128)(2,1)S(1)}, u32[]{:S(2)}, u32[]{:S(2)}) %all-to-all-start) | async-done | bytes 2097184 | tf_op jit(solution)/shard_map/all_to_all | solution.py:20
  128.1 11.3 %all-to-all-start.1 = ((bf16[128,64,256]{2,0,1:T(8,128)(2,1)}), bf16[128,64,256]{2,0,1:T(8,128)(2,1)}, u32[]{:S(2)}, u32[]{:S(2)}) async-start(bf16[128,64,256]{2,0,1:T(8,128)(2,1)} %pad_maximum_fusion), calls=%async_computation.1 | async-start | bytes 8388608 | tf_op jit(solution)/shard_map/all_to_all | solution.py:20
  139.7 0.7 dynamic-slice_bitcast_fusion.1
  140.4 0.8 gather_fusion
  141.6 0.6 gather_fusion.1
  143.0 1.0 slice_bitcast_fusion.1
  144.1 177.6 %all-to-all-done.1 = bf16[128,64,256]{2,0,1:T(8,128)(2,1)} async-done(((bf16[128,64,256]{2,0,1:T(8,128)(2,1)}), bf16[128,64,256]{2,0,1:T(8,128)(2,1)}, u32[]{:S(2)}, u32[]{:S(2)}) %all-to-all-start.1) | async-done | bytes 4194336 | tf_op jit(solution)/shard_map/all_to_all | solution.py:20
  321.7 3.8 fusion.46
  325.5 4.6 gather_fusion.6
  330.1 3.1 gather_fusion.5
  333.2 3.9 broadcast_select_fusion.1
  337.1 1.6 fusion.18
  338.7 11.4 %fusion.48 = (f32[64,64]{1,0:T(8,128)S(1)}, f32[64,64,256]{2,1,0:T(8,128)S(1)}) fusion(f32[64,64,256]{2,1,0:T(8,128)S(1)} %fusion.18, pred[64,256]{1,0:T(8,128)(4,1)S(1)} %bitcast.142), kind=kOutput, calls=%fused_computation.112 | output fusion | flops 6291711 | bytes 8421376 | tf_op jit(solution)/shard_map/sub | solution.py:53
  350.1 1.4 multiply_reduce_fusion
  351.5 0.5 copy-done.11
  352.0 2.0 multiply_convert_fusion
  354.1 0.9 convolution_multiply_fusion
  355.7 1.1 copy.74
  356.9 13.0 %all-to-all-start.2 = ((bf16[64,32,2,128]{3,1,2,0:T(8,128)(2,1)}), bf16[64,32,2,128]{3,1,2,0:T(8,128)(2,1)}, u32[]{:S(2)}, u32[]{:S(2)}) async-start(bf16[64,32,2,128]{3,1,2,0:T(8,128)(2,1)} %copy.74), calls=%async_computation.2 | async-start | bytes 2097152 | tf_op jit(solution)/shard_map/all_to_all | solution.py:160
  370.1 3.0 broadcast_multiply_fusion
  373.2 2.4 fusion.21
  375.6 10.7 %fusion.13 = bf16[64,128,128]{2,0,1:T(8,128)(2,1)S(1)} fusion(f32[128,128,128]{2,1,0:T(8,128)S(1)} %bitcast.118, s32[128]{0:T(128)S(1)} %select_n.156), kind=kOutput, calls=%fused_computation.33 | convolution fusion | flops 1611669504 | bytes 10486272 | tf_op jit(solution)/shard_map/mn,mrd->nrd/dot_general | solution.py:83
  386.3 10.9 %fusion.10 = bf16[64,128,128]{2,0,1:T(8,128)(2,1)S(1)} fusion(f32[128,128,128]{2,1,0:T(8,128)S(1)} %bitcast.113, s32[128]{0:T(128)S(1)} %select_n.156), kind=kOutput, calls=%fused_computation.32 | convolution fusion | flops 1611669504 | bytes 10486272 | tf_op jit(solution)/shard_map/mn,mrd->nrd/dot_general | solution.py:76
  397.6 4.7 copy.78
  402.2 17.7 %all-to-all-done.2 = bf16[64,32,2,128]{3,1,2,0:T(8,128)(2,1)} async-done(((bf16[64,32,2,128]{3,1,2,0:T(8,128)(2,1)}), bf16[64,32,2,128]{3,1,2,0:T(8,128)(2,1)}, u32[]{:S(2)}, u32[]{:S(2)}) %all-to-all-start.2) | async-done | bytes 1048608 | tf_op jit(solution)/shard_map/all_to_all | solution.py:160
  419.9 10.3 %all-to-all-start.3 = ((bf16[64,256,128]{2,1,0:T(8,128)(2,1)}), bf16[64,256,128]{2,1,0:T(8,128)(2,1)}, u32[]{:S(2)}, u32[]{:S(2)}) async-start(bf16[64,256,128]{2,1,0:T(8,128)(2,1)} %copy.78), calls=%async_computation.3 | async-start | bytes 8388608 | tf_op jit(solution)/shard_map/all_to_all | solution.py:20
  430.6 1.0 fusion.28
  431.7 58.0 %all-reduce.5.cloned.1.call-done = f32[128,128]{1,0:T(8,128)} async-done(((f32[128,128]{1,0:T(8,128)}), f32[128,128]{1,0:T(8,128)}) %all-reduce.5.cloned.1.call-update) | async-done | bytes 65552 | tf_op jit(solution)/shard_map/psum | solution.py:25
  489.8 152.9 %all-reduce.7.cloned.1.call-done = f32[128,128]{1,0:T(8,128)} async-done(((f32[128,128]{1,0:T(8,128)}), f32[128,128]{1,0:T(8,128)}) %all-reduce.7.cloned.1.call-update) | async-done | bytes 65552 | tf_op jit(solution)/shard_map/psum | solution.py:25
  642.8 61.4 %all-reduce.9.cloned.1.call-done = f32[128,128]{1,0:T(8,128)} async-done(((f32[128,128]{1,0:T(8,128)}), f32[128,128]{1,0:T(8,128)}) %all-reduce.9.cloned.1.call-update) | async-done | bytes 65552 | tf_op jit(solution)/shard_map/psum | solution.py:25
  704.3 45.7 %all-reduce.11.cloned.1.call-done = f32[32,4,128]{2,1,0:T(4,128)} async-done(((f32[32,4,128]{2,1,0:T(4,128)}), f32[32,4,128]{2,1,0:T(4,128)}) %all-reduce.11.cloned.1.call-update) | async-done | bytes 65552 | tf_op jit(solution)/shard_map/psum | solution.py:25
  749.9 1.5 reduce_sum.85
  751.4 2.0 gather_fusion.2
  753.6 0.7 copy.75
  754.3 1.3 reshape.254
  755.6 2.9 bitcast_reduce_fusion
  758.6 0.8 copy.82
  759.5 0.8 copy.81
  (78 shorter events, 5.2 us)
Async XLA Ops:
  7.2 134.3 %copy-start = (s32[32,64,2]{1,2,0:T(2,128)S(1)}, s32[32,64,2]{1,2,0:T(2,128)}, u32[]{:S(2)}) copy-start(s32[32,64,2]{1,2,0:T(2,128)} %param.16) | copy-start | bytes 49156
  7.2 2.1 copy-start.3
  9.3 0.7 copy-start.10
  12.5 20.9 %copy-start.8 = (bf16[1,128,512]{2,1,0:T(8,128)(2,1)S(1)}, bf16[1,128,512]{2,1,0:T(8,128)(2,1)}, u32[]{:S(2)}) copy-start(bf16[1,128,512]{2,1,0:T(8,128)(2,1)} %param.12) | copy-start | bytes 393220
  12.5 20.9 %copy-start.9 = (bf16[1,128,512]{2,1,0:T(8,128)(2,1)S(1)}, bf16[1,128,512]{2,1,0:T(8,128)(2,1)}, u32[]{:S(2)}) copy-start(bf16[1,128,512]{2,1,0:T(8,128)(2,1)} %param.13) | copy-start | bytes 393220
  14.0 114.1 %all-to-all-start = ((bf16[32,64,4,128]{3,0,2,1:T(8,128)(2,1)}), bf16[32,64,4,128]{3,0,2,1:T(8,128)(2,1)S(1)}, u32[]{:S(2)}, u32[]{:S(2)}) async-start(bf16[32,64,4,128]{3,0,2,1:T(8,128)(2,1)} %pad_maximum_fusion.2), calls=%async_computation | async-start | bytes 4194304 | tf_op jit(solution)/shard_map/all_to_all | solution.py:20
  128.1 193.6 %all-to-all-start.1 = ((bf16[128,64,256]{2,0,1:T(8,128)(2,1)}), bf16[128,64,256]{2,0,1:T(8,128)(2,1)}, u32[]{:S(2)}, u32[]{:S(2)}) async-start(bf16[128,64,256]{2,0,1:T(8,128)(2,1)} %pad_maximum_fusion), calls=%async_computation.1 | async-start | bytes 8388608 | tf_op jit(solution)/shard_map/all_to_all | solution.py:20
  338.7 11.4 %copy-start.4 = (bf16[64,32,128]{2,1,0:T(8,128)(2,1)S(1)}, bf16[64,32,128]{2,1,0:T(8,128)(2,1)}, u32[]{:S(2)}) copy-start(bf16[64,32,128]{2,1,0:T(8,128)(2,1)} %get-tuple-element.30) | copy-start | bytes 1572868
  338.7 11.4 %copy-start.6 = (bf16[64,32,128]{2,1,0:T(8,128)(2,1)S(1)}, bf16[64,32,128]{2,1,0:T(8,128)(2,1)}, u32[]{:S(2)}) copy-start(bf16[64,32,128]{2,1,0:T(8,128)(2,1)} %get-tuple-element.31) | copy-start | bytes 1572868
  350.1 1.9 copy-start.11
  354.1 1.3 copy-start.2
  356.9 63.1 %all-to-all-start.2 = ((bf16[64,32,2,128]{3,1,2,0:T(8,128)(2,1)}), bf16[64,32,2,128]{3,1,2,0:T(8,128)(2,1)}, u32[]{:S(2)}, u32[]{:S(2)}) async-start(bf16[64,32,2,128]{3,1,2,0:T(8,128)(2,1)} %copy.74), calls=%async_computation.2 | async-start | bytes 2097152 | tf_op jit(solution)/shard_map/all_to_all | solution.py:160
  370.0 3.1 copy-start.5
  370.0 3.1 copy-start.7
  370.1 3.1 copy-start.12
  419.9 335.7 %all-to-all-start.3 = ((bf16[64,256,128]{2,1,0:T(8,128)(2,1)}), bf16[64,256,128]{2,1,0:T(8,128)(2,1)}, u32[]{:S(2)}, u32[]{:S(2)}) async-start(bf16[64,256,128]{2,1,0:T(8,128)(2,1)} %copy.78), calls=%async_computation.3 | async-start | bytes 8388608 | tf_op jit(solution)/shard_map/all_to_all | solution.py:20
  430.2 59.5 %all-reduce.5.cloned.1.call-start = ((), (), s32[]{:S(2)}) async-start(), calls=%async_computation.4 | async-start | bytes 131072 | tf_op jit(solution)/shard_map/psum | solution.py:25
  431.5 211.2 %all-reduce.7.cloned.1.call-start = ((), (), s32[]{:S(2)}) async-start(), calls=%async_computation.5 | async-start | bytes 131072 | tf_op jit(solution)/shard_map/psum | solution.py:25
  489.7 214.5 %all-reduce.9.cloned.1.call-start = ((), (), s32[]{:S(2)}) async-start(), calls=%async_computation.6 | async-start | bytes 131072 | tf_op jit(solution)/shard_map/psum | solution.py:25
  642.7 107.2 %all-reduce.11.cloned.1.call-start = ((), (), s32[]{:S(2)}) async-start(), calls=%async_computation.7 | async-start | bytes 131072 | tf_op jit(solution)/shard_map/psum | solution.py:25
  753.6 6.7 copy-start.1
Sparse Core Ops, SparseCore 0:
  433.9 55.7 all-reduce.4
  492.1 150.5 all-reduce.6
  645.0 59.1 all-reduce.8
  707.2 42.7 all-reduce.10
where the time goes:
time: 768 us; the launch traced here: 767 us
  waiting for transfers between devices  604 us (79%)
  starting transfers between devices  54.1 us (7%)
  local copies, waits for them, and re-layouts  34.1 us (4%)
  matrix products  34 us (4%)
  other arithmetic  25.9 us (3%)
  between operations  14.5 us (2%)
    psum x4, waiting for transfers between devices, one_axis_at_a_time(): return functools.reduce(lax.psum, axes, x)  318 us
    all_to_all x3, waiting for transfers between devices, in_one_piece(): lax.all_to_all(both, axis, split_axis=split_dim, concat_axis=concat_dim,...  269 us
    all_to_all x3, starting transfers between devices, in_one_piece(): lax.all_to_all(both, axis, split_axis=split_dim, concat_axis=concat_dim,...  40.9 us
    all_to_all x1, waiting for transfers between devices, body(): lax.all_to_all(dq_send, SEQ, split_axis=0, concat_axis=0, tiled=True)  17.7 us
  transfers between devices with their start and end apart: 8, of which 7 were waited for; matrix products, arithmetic and copies ran while one was open for 6% of the time, Pallas kernels for 0%

commit v1 on v0

v1 whole, which is shorter than its diff:
```python
import functools

import jax
import jax.numpy as jnp
from jax import lax
from jax.experimental import pallas as pl
from jax.experimental.pallas import tpu as pltpu
from jax.sharding import Mesh
from jax.sharding import PartitionSpec as P

SEQ = ("y", "z")
REP = ("x", "core")
HEAD = 128
BLOCK = 128
GROUP = 8
NEG = -1e30


def dot(a, b, ca, cb):
    return lax.dot_general(a, b, (((ca,), (cb,)), ((), ())), preferred_element_type=jnp.float32)


def attend_kernel(
    other_ref, count_ref, own_ref, kv_ref, q_ref, g_ref, dq_ref, dkv_ref, dbq_ref, acc_ref
):
    step = pl.program_id(0)
    scaling = HEAD**-0.5

    @pl.when(step == 0)
    def _():
        acc_ref[...] = jnp.zeros_like(acc_ref)
        dbq_ref[...] = jnp.zeros_like(dbq_ref)

    own = own_ref[step]
    key_own = kv_ref[own, 0]
    value_own = kv_ref[own, 1]
    key_position = lax.broadcasted_iota(jnp.int32, (2 * BLOCK, 1), 0)
    dk_own = jnp.zeros((BLOCK, HEAD), jnp.float32)
    dv_own = jnp.zeros((BLOCK, HEAD), jnp.float32)
    for h in range(GROUP):
        other = other_ref[h, step]
        limit = count_ref[h, step] * BLOCK
        cols = slice(h * HEAD, (h + 1) * HEAD)
        q = q_ref[0, :, cols]
        g = g_ref[0, :, cols]
        keys = jnp.concatenate([key_own, kv_ref[other, 0]], axis=0)
        values = jnp.concatenate([value_own, kv_ref[other, 1]], axis=0)
        scores = dot(keys, q, 1, 1) * scaling
        scores = jnp.where(key_position < limit, scores, NEG)
        top = jnp.max(scores, axis=0, keepdims=True)
        raised = jnp.exp(scores - top)
        weights = raised / jnp.sum(raised, axis=0, keepdims=True)
        weights_half = weights.astype(jnp.bfloat16)
        weight_grads = dot(values, g, 1, 1)
        row_dots = jnp.sum(weights_half.astype(jnp.float32) * weight_grads, axis=0, keepdims=True)
        score_grads = (weights * (weight_grads - row_dots)).astype(jnp.bfloat16)
        grad_q = scaling * dot(score_grads, keys, 0, 0)
        dk = scaling * dot(score_grads, q, 1, 0)
        dv = dot(weights_half, g, 1, 0)
        dq_ref[0, :, cols] = grad_q.astype(jnp.bfloat16)
        dbq_ref[h : h + 1, :] += jnp.sum(grad_q, axis=0, keepdims=True)
        dk_own += dk[:BLOCK]
        dv_own += dv[:BLOCK]
        acc_ref[other, 0] += dk[BLOCK:]
        acc_ref[other, 1] += dv[BLOCK:]
    acc_ref[own, 0] += dk_own
    acc_ref[own, 1] += dv_own

    @pl.when(step == pl.num_programs(0) - 1)
    def _():
        @pl.loop(0, acc_ref.shape[0])
        def _(n):
            dkv_ref[n] = acc_ref[n].astype(jnp.bfloat16)


def attend(other, counts, own, kv, q, g):
    blocks, rows, width = q.shape
    tiles = kv.shape[0]
    per_block = pl.BlockSpec((1, rows, width), lambda i, *_: (i, 0, 0))
    whole = pl.BlockSpec(kv.shape, lambda i, *_: (0, 0, 0, 0))
    return pl.pallas_call(
        attend_kernel,
        grid_spec=pltpu.PrefetchScalarGridSpec(
            num_scalar_prefetch=3,
            grid=(blocks,),
            in_specs=[whole, per_block, per_block],
            out_specs=[per_block, whole, pl.BlockSpec((GROUP, HEAD), lambda i, *_: (0, 0))],
            scratch_shapes=[pltpu.VMEM(kv.shape, jnp.float32)],
        ),
        out_shape=[
            jax.ShapeDtypeStruct(q.shape, jnp.bfloat16),
            jax.ShapeDtypeStruct(kv.shape, jnp.bfloat16),
            jax.ShapeDtypeStruct((GROUP, HEAD), jnp.float32),
        ],
        compiler_params=pltpu.CompilerParams(
            dimension_semantics=("arbitrary",), vmem_limit_bytes=48 * 1024 * 1024
        ),
        cost_estimate=pl.CostEstimate(
            flops=14 * blocks * GROUP * rows * 2 * BLOCK * HEAD,
            bytes_accessed=14 * 1024 * 1024,
            transcendentals=blocks * GROUP * rows * 2 * BLOCK,
        ),
    )(other, counts, own, kv, q, g)


def by_group(x, groups):
    rows, width = x.shape
    return jnp.transpose(x.reshape(rows, groups, width // groups), (1, 0, 2))


def side_by_side(x):
    groups, rows, width = x.shape
    return jnp.transpose(x, (1, 0, 2)).reshape(rows, groups * width)


def body(q_lin, k_lin, value_projection, grad_out, q_bias, block_lists, block_counts):
    my_y = lax.axis_index("y")
    my_z = lax.axis_index("z")
    y_size = lax.axis_size("y")
    z_size = lax.axis_size("z")
    groups = y_size
    exchange = functools.partial(
        lax.all_to_all, axis_name="y", split_axis=0, concat_axis=0, tiled=True
    )

    kv_mine = jnp.stack([by_group(k_lin[0], groups), by_group(value_projection[0], groups)], axis=1)
    kv_head = exchange(kv_mine)
    kv_all = lax.all_gather(kv_head, "z", axis=0, tiled=True)

    query_rows = (q_lin[0].astype(jnp.float32) + q_bias).astype(jnp.bfloat16)
    qg = jnp.stack([by_group(query_rows, groups), by_group(grad_out[0], groups)], axis=1)
    qg, kv_head = lax.optimization_barrier((qg, kv_head))
    got = exchange(qg)
    got_q, got_g = got[:, 0], got[:, 1]

    mine = (GROUP, y_size, z_size)
    lists = lax.dynamic_slice_in_dim(block_lists[:, :, 1], my_y * GROUP, GROUP, axis=0)
    lists = lax.dynamic_index_in_dim(lists.reshape(mine), my_z, 2, keepdims=False)
    counts = lax.dynamic_slice_in_dim(block_counts, my_y * GROUP, GROUP, axis=0)
    counts = lax.dynamic_index_in_dim(counts.reshape(mine), my_z, 2, keepdims=False)
    other = lists % z_size * y_size + lists // z_size
    own = my_z * y_size + jnp.arange(y_size, dtype=jnp.int32)

    dq_head, dkv_all, dbq_part = attend(other, counts, own, kv_all, got_q, got_g)

    dkv_head = lax.psum_scatter(dkv_all, "z", scatter_dimension=0, tiled=True)
    dq_out = side_by_side(exchange(dq_head))[None]
    dbq_z = jnp.sum(lax.all_gather(dbq_part, "z", axis=0), axis=0)
    dbq_head = jnp.sum(lax.all_gather(dbq_z, REP, axis=0), axis=0)
    dbq_out = lax.all_gather(dbq_head, "y", axis=0, tiled=True).reshape(-1)

    dkv_mine = exchange(dkv_head)
    dk_out = side_by_side(dkv_mine[:, 0])[None]
    dv_out = side_by_side(dkv_mine[:, 1])[None]
    return dq_out, dk_out, dv_out, dbq_out


def solution(mesh):
    torus = Mesh(mesh.devices.reshape(4, 16, 4, 2), ("y", "z", "x", "core"))
    split = P(REP, SEQ, None)
    return jax.shard_map(
        body,
        mesh=torus,
        in_specs=(split, split, split, split, P(), P(), P()),
        out_specs=(split, split, split, P()),
        check_vma=False,
    )
```

time: 768 us -> 238 us (0.31)
  the two profiles are of different devices: /device:TPU:1 before, /device:TPU:2 now
where the time goes in v1:
time: 238 us
  waiting for transfers between devices  112 us (47%)
  blocking collectives  65.9 us (28%)
  Pallas kernels  17.2 us (7%)
  between operations  14.2 us (6%)
  local copies, waits for them, and re-layouts  13.9 us (6%)
  starting transfers between devices  13.2 us (6%)
    all_gather x1, waiting for transfers between devices, body(): kv_all = lax.all_gather(kv_head, 'z', axis=0, tiled=True)  44.6 us
    reduce_scatter x1, waiting for transfers between devices, body(): dkv_head = lax.psum_scatter(dkv_all, 'z', scatter_dimension=0, tiled=True)  43.4 us
    all_gather x1, blocking collectives, body(): dbq_z = jnp.sum(lax.all_gather(dbq_part, 'z', axis=0), axis=0)  29 us
    all_to_all x1, waiting for transfers between devices, body(): got = exchange(qg)  24.5 us
    pallas_call x1, Pallas kernels, attend(): pl.pallas_call(attend_kernel, grid_spec=pltpu.PrefetchScalarGridSpec(num_...  17.2 us
    all_gather x1, blocking collectives, body(): dbq_head = jnp.sum(lax.all_gather(dbq_z, REP, axis=0), axis=0)  13 us
    all_gather x1, blocking collectives, body(): dbq_out = lax.all_gather(dbq_head, 'y', axis=0, tiled=True).reshape(-1)  12.8 us
    all_to_all x1, blocking collectives, body(): kv_head = exchange(kv_mine)  11.1 us
  transfers between devices with their start and end apart: 5, of which 3 were waited for; matrix products, arithmetic and copies ran while one was open for 4% of the time, Pallas kernels for 0%

profile of v1, /device:TPU:2, one launch (start us, length us, event | category | flops | bytes accessed | tf_op | source)
XLA Modules:
  0.0 237.8 jit_solution(13412966789583459223)
XLA Ops:
  7.2 0.0 copy-start
  7.2 0.0 copy-start.3
  7.2 0.0 copy-start.1
  7.2 0.0 all-gather.4.cloned.1.call-start
  7.2 1.1 copy.86
  8.4 1.0 copy.87
  9.4 0.0 copy-start.2
  9.5 11.1 %all_to_all.20 = bf16[4,2,128,128]{2,3,1,0:T(8,128)(2,1)S(1)} all-to-all(bf16[4,2,128,128]{2,3,1,0:T(8,128)(2,1)S(1)} %copy.88), channel_id=1, replica_groups=mesh['y'=4,'z'=16,'x'=4,'core'=2] {'y'}, dimensions={0} | all-to-all | bytes 524288 | tf_op jit(solution)/shard_map/all_to_all | solution.py:127
  20.5 0.8 copy.89
  21.4 0.0 all-gather.4.cloned.1.call-update
  21.4 0.0 copy-done.3
  21.4 0.0 copy-done.1
  21.4 0.7 copy.90
  22.1 0.0 copy-done.2
  22.1 0.7 copy.91
  22.8 0.7 fusion.1
  23.5 0.2 pad_maximum_fusion
  23.7 2.7 %copy.92 = bf16[4,2,128,1024]{3,2,1,0:T(8,128)(2,1)} copy(bf16[4,2,128,1024]{2,3,0,1:T(8,128)(2,1)S(1)} %pad_maximum_fusion) | data formatting | bytes 4194304 | tf_op jit(solution)/shard_map/optimization_barrier | solution.py:132
  26.4 4.6 %all-to-all-start.1 = ((bf16[4,2,128,1024]{3,2,1,0:T(8,128)(2,1)}), bf16[4,2,128,1024]{3,2,1,0:T(8,128)(2,1)}, u32[]{:S(2)}, u32[]{:S(2)}) async-start(bf16[4,2,128,1024]{3,2,1,0:T(8,128)(2,1)} %copy.92), calls=%async_computation.1 | async-start | bytes 4194304 | tf_op jit(solution)/shard_map/all_to_all | solution.py:133
  31.0 0.0 reduce-scatter.2.cloned.1.call-start
  31.1 0.1 reshape.30
  31.2 0.0 copy-done.4
  31.2 0.1 reshape.29
  31.3 0.1 constant_dynamic-slice_fusion
  31.4 0.1 copy.85
  31.5 0.1 copy.95.count_ref
  31.6 0.1 copy.80
  31.7 0.1 copy.81
  31.8 24.5 %all-to-all-done.1 = bf16[4,2,128,1024]{3,2,1,0:T(8,128)(2,1)} async-done(((bf16[4,2,128,1024]{3,2,1,0:T(8,128)(2,1)}), bf16[4,2,128,1024]{3,2,1,0:T(8,128)(2,1)}, u32[]{:S(2)}, u32[]{:S(2)}) %all-to-all-start.1) | async-done | bytes 2097184 | tf_op jit(solution)/shard_map/all_to_all | solution.py:133
  56.3 1.7 slice_bitcast_fusion
  58.0 44.6 %all-gather.4.cloned.1.call-done.kv_ref = bf16[64,2,128,128]{3,2,1,0:T(8,128)(2,1)} async-done(((bf16[4,2,128,128]{3,2,1,0:T(8,128)(2,1)}), bf16[64,2,128,128]{3,2,1,0:T(8,128)(2,1)}) %all-gather.4.cloned.1.call-update) | async-done | bytes 4194320 | tf_op jit(solution)/shard_map/all_gather | solution.py:128
  102.6 17.2 %shard_map.102 = (bf16[4,128,1024]{2,1,0:T(8,128)(2,1)}, bf16[64,2,128,128]{3,2,1,0:T(8,128)(2,1)}, f32[8,128]{1,0:T(8,128)S(1)}) custom-call(s32[8,4]{1,0:T(8,128)S(1)} %fusion.3.other_ref, s32[8,4]{1,0:T(8,128)S(1)} %copy.95.count_ref, s32[4]{0:T(128)S(1)} %iota_add_fusion.own_ref, bf16[64,2,128,128]{3,2,1,0:T(8,128)(2,1)} %all-gather.4.cloned.1.call-done.kv_ref, ...), custom_call_target="tpu_custom_call" | custom-call | flops 1879048192 | bytes 14680064 | tf_op jit(solution)/shard_map/pallas_call | solution.py:81
  119.7 0.0 reduce-scatter.2.cloned.1.call-update
  119.8 4.5 %all-to-all-start.2 = ((bf16[4,128,1024]{2,1,0:T(8,128)(2,1)}), bf16[4,128,1024]{2,1,0:T(8,128)(2,1)S(1)}, u32[]{:S(2)}, u32[]{:S(2)}) async-start(bf16[4,128,1024]{2,1,0:T(8,128)(2,1)} %get-tuple-element.9), calls=%async_computation.2 | async-start | bytes 2097152 | tf_op jit(solution)/shard_map/all_to_all | solution.py:147
  124.2 29.0 %all-gather = f32[128,128]{1,0:T(8,128)S(1)} all-gather(f32[8,128]{1,0:T(8,128)S(1)} %get-tuple-element.11), channel_id=2, replica_groups=mesh['y'=4,'z'=16,'x'=4,'core'=2] {'z'}, dimensions={0}, use_global_device_ids=true | all-gather | bytes 69632 | tf_op jit(solution)/shard_map/all_gather | solution.py:148
  153.2 0.0 all-to-all-done.2
  153.2 43.4 %reduce-scatter.2.cloned.1.call-done = bf16[4,2,128,128]{3,2,1,0:T(8,128)(2,1)} async-done(((bf16[64,2,128,128]{3,2,1,0:T(8,128)(2,1)}), bf16[4,2,128,128]{3,2,1,0:T(8,128)(2,1)}) %reduce-scatter.2.cloned.1.call-update) | async-done | bytes 262160 | tf_op jit(solution)/shard_map/reduce_scatter | solution.py:146
  196.6 4.0 %all-to-all-start.3 = ((bf16[4,2,128,128]{3,2,1,0:T(8,128)(2,1)}), bf16[4,2,128,128]{3,2,1,0:T(8,128)(2,1)S(1)}, u32[]{:S(2)}, u32[]{:S(2)}) async-start(bf16[4,2,128,128]{3,2,1,0:T(8,128)(2,1)} %reduce-scatter.2.cloned.1.call-done), calls=%async_computation.4 | async-start | bytes 524288 | tf_op jit(solution)/shard_map/all_to_all | solution.py:152
  200.7 13.0 %all-gather.1 = f32[64,128]{1,0:T(8,128)S(1)} all-gather(f32[8,128]{1,0:T(8,128)S(1)} %bitcast_reduce_fusion), channel_id=3, replica_groups=mesh['y'=4,'z'=16,'x'=4,'core'=2] {'x','core'}, dimensions={0}, use_global_device_ids=true | all-gather | bytes 36864 | tf_op jit(solution)/shard_map/all_gather | solution.py:149
  213.7 12.8 %all_gather.23 = f32[32,128]{1,0:T(8,128)S(1)} all-gather(f32[8,128]{1,0:T(8,128)S(1)} %bitcast_reduce_fusion.1), channel_id=1, replica_groups=mesh['y'=4,'z'=16,'x'=4,'core'=2] {'y'}, dimensions={0}, use_global_device_ids=true | all-gather | bytes 20480 | tf_op jit(solution)/shard_map/all_gather | solution.py:150
  226.5 0.7 copy.96
  227.2 1.3 copy.99
  228.5 0.0 all-to-all-done.3
  228.5 0.1 copy.98
  228.7 0.8 copy.101
  229.4 0.1 copy.97
  229.6 0.8 copy.100
  230.3 0.6 copy.105
  (13 shorter events, 0.2 us)
Async XLA Ops:
  7.2 23.9 %copy-start = (s32[32,64]{1,0:T(8,128)S(1)}, s32[32,64]{1,0:T(8,128)}, u32[]{:S(2)}) copy-start(s32[32,64]{1,0:T(8,128)} %param.13) | copy-start | bytes 24580
  7.2 14.2 %copy-start.3 = (f32[4096]{0:T(1024)S(1)}, f32[4096]{0:T(1024)}, u32[]{:S(2)}) copy-start(f32[4096]{0:T(1024)} %param.11) | copy-start | bytes 49156
  7.2 14.2 %copy-start.1 = (bf16[1,128,4096]{2,1,0:T(8,128)(2,1)S(1)}, bf16[1,128,4096]{2,1,0:T(8,128)(2,1)}, u32[]{:S(2)}) copy-start(bf16[1,128,4096]{2,1,0:T(8,128)(2,1)} %param.7) | copy-start | bytes 3145732
  7.2 95.4 %all-gather.4.cloned.1.call-start = ((), (), s32[]{:S(2)}) async-start(), calls=%async_computation.5 | async-start | bytes 4456448 | tf_op jit(solution)/shard_map/all_gather | solution.py:128
  9.4 12.7 %copy-start.2 = (bf16[1,128,4096]{2,1,0:T(8,128)(2,1)S(1)}, bf16[1,128,4096]{2,1,0:T(8,128)(2,1)}, u32[]{:S(2)}) copy-start(bf16[1,128,4096]{2,1,0:T(8,128)(2,1)} %param.10) | copy-start | bytes 3145732
  26.4 4.8 %copy-start.4 = (s32[32,64,2]{1,2,0:T(2,128)S(1)}, s32[32,64,2]{1,2,0:T(2,128)}, u32[]{:S(2)}) copy-start(s32[32,64,2]{1,2,0:T(2,128)} %param.12) | copy-start | bytes 49156
  26.4 29.9 %all-to-all-start.1 = ((bf16[4,2,128,1024]{3,2,1,0:T(8,128)(2,1)}), bf16[4,2,128,1024]{3,2,1,0:T(8,128)(2,1)}, u32[]{:S(2)}, u32[]{:S(2)}) async-start(bf16[4,2,128,1024]{3,2,1,0:T(8,128)(2,1)} %copy.92), calls=%async_computation.1 | async-start | bytes 4194304 | tf_op jit(solution)/shard_map/all_to_all | solution.py:133
  31.0 165.6 %reduce-scatter.2.cloned.1.call-start = ((), (), s32[]{:S(2)}) async-start(), calls=%async_computation.6 | async-start | bytes 4456448 | tf_op jit(solution)/shard_map/reduce_scatter | solution.py:146
  119.8 33.4 %all-to-all-start.2 = ((bf16[4,128,1024]{2,1,0:T(8,128)(2,1)}), bf16[4,128,1024]{2,1,0:T(8,128)(2,1)S(1)}, u32[]{:S(2)}, u32[]{:S(2)}) async-start(bf16[4,128,1024]{2,1,0:T(8,128)(2,1)} %get-tuple-element.9), calls=%async_computation.2 | async-start | bytes 2097152 | tf_op jit(solution)/shard_map/all_to_all | solution.py:147
  196.6 31.9 %all-to-all-start.3 = ((bf16[4,2,128,128]{3,2,1,0:T(8,128)(2,1)}), bf16[4,2,128,128]{3,2,1,0:T(8,128)(2,1)S(1)}, u32[]{:S(2)}, u32[]{:S(2)}) async-start(bf16[4,2,128,128]{3,2,1,0:T(8,128)(2,1)} %reduce-scatter.2.cloned.1.call-done), calls=%async_computation.4 | async-start | bytes 524288 | tf_op jit(solution)/shard_map/all_to_all | solution.py:152
Sparse Core Ops, SparseCore 0:
  21.5 80.9 all-gather.3
  119.9 76.7 reduce-scatter.1

commit v2 on v1

v2 whole, which is shorter than its diff:
```python
import functools

import jax
import jax.numpy as jnp
from jax import lax
from jax.experimental import pallas as pl
from jax.experimental.pallas import tpu as pltpu
from jax.sharding import Mesh
from jax.sharding import PartitionSpec as P

SEQ = ("y", "z")
REP = ("x", "core")
HEAD = 128
BLOCK = 128
GROUP = 8
NEG = -1e30


def dot(a, b, ca, cb):
    return lax.dot_general(a, b, (((ca,), (cb,)), ((), ())), preferred_element_type=jnp.float32)


def attend_kernel(
    other_ref, count_ref, own_ref, kv_ref, qg_ref, dq_ref, dkv_ref, dbq_ref, acc_ref
):
    step = pl.program_id(0)
    scaling = HEAD**-0.5

    @pl.when(step == 0)
    def _():
        acc_ref[...] = jnp.zeros_like(acc_ref)
        dbq_ref[...] = jnp.zeros_like(dbq_ref)

    heads = range(GROUP)
    cols = [slice(h * HEAD, (h + 1) * HEAD) for h in heads]
    own = own_ref[step]
    others = [other_ref[h, step] for h in heads]
    q = [qg_ref[0, 0, :, c] for c in cols]
    g = [qg_ref[0, 1, :, c] for c in cols]
    q_all = jnp.concatenate(q, axis=0)
    g_all = jnp.concatenate(g, axis=0)
    key_own = kv_ref[own, 0]
    value_own = kv_ref[own, 1]
    key_other = [kv_ref[n, 0] for n in others]
    value_other = [kv_ref[n, 1] for n in others]

    scores_own = dot(key_own, q_all, 1, 1)
    scores_other = jnp.concatenate([dot(key_other[h], q[h], 1, 1) for h in heads], axis=1)
    closed = jnp.concatenate(
        [jnp.full((1, BLOCK), jnp.where(count_ref[h, step] > 1, 0.0, NEG)) for h in heads], axis=1
    )
    scores_other = scores_other + closed
    top = jnp.maximum(
        jnp.max(scores_own, axis=0, keepdims=True), jnp.max(scores_other, axis=0, keepdims=True)
    )
    raised_own = jnp.exp((scores_own - top) * scaling)
    raised_other = jnp.exp((scores_other - top) * scaling)
    share = 1.0 / (
        jnp.sum(raised_own, axis=0, keepdims=True) + jnp.sum(raised_other, axis=0, keepdims=True)
    )
    weights_own = raised_own * share
    weights_other = raised_other * share
    half_own = weights_own.astype(jnp.bfloat16)
    half_other = weights_other.astype(jnp.bfloat16)
    wg_own = dot(value_own, g_all, 1, 1)
    wg_other = jnp.concatenate([dot(value_other[h], g[h], 1, 1) for h in heads], axis=1)
    row_dots = jnp.sum(half_own.astype(jnp.float32) * wg_own, axis=0, keepdims=True) + jnp.sum(
        half_other.astype(jnp.float32) * wg_other, axis=0, keepdims=True
    )
    sg_own = (weights_own * (wg_own - row_dots)).astype(jnp.bfloat16)
    sg_other = (weights_other * (wg_other - row_dots)).astype(jnp.bfloat16)
    dk_own = dot(sg_own, q_all, 1, 0)
    dv_own = dot(half_own, g_all, 1, 0)
    sums = []
    for h in heads:
        grad_q = scaling * dot(
            jnp.concatenate([sg_own[:, cols[h]], sg_other[:, cols[h]]], axis=0),
            jnp.concatenate([key_own, key_other[h]], axis=0),
            0,
            0,
        )
        dq_ref[0, :, cols[h]] = grad_q.astype(jnp.bfloat16)
        sums.append(jnp.sum(grad_q, axis=0, keepdims=True))
    dbq_ref[...] += jnp.concatenate(sums, axis=0)
    dk_other = [dot(sg_other[:, cols[h]], q[h], 1, 0) for h in heads]
    dv_other = [dot(half_other[:, cols[h]], g[h], 1, 0) for h in heads]
    acc_ref[own, 0] += dk_own
    acc_ref[own, 1] += dv_own
    for h in heads:
        acc_ref[others[h], 0] += dk_other[h]
        acc_ref[others[h], 1] += dv_other[h]

    @pl.when(step == pl.num_programs(0) - 1)
    def _():
        @pl.loop(0, acc_ref.shape[0])
        def _(n):
            dkv_ref[n, 0] = (acc_ref[n, 0] * scaling).astype(jnp.bfloat16)
            dkv_ref[n, 1] = acc_ref[n, 1].astype(jnp.bfloat16)


def attend(other, counts, own, kv, qg):
    blocks, _, rows, width = qg.shape
    whole = pl.BlockSpec(kv.shape, lambda i, *_: (0, 0, 0, 0))
    return pl.pallas_call(
        attend_kernel,
        grid_spec=pltpu.PrefetchScalarGridSpec(
            num_scalar_prefetch=3,
            grid=(blocks,),
            in_specs=[whole, pl.BlockSpec((1, 2, rows, width), lambda i, *_: (i, 0, 0, 0))],
            out_specs=[
                pl.BlockSpec((1, rows, width), lambda i, *_: (i, 0, 0)),
                whole,
                pl.BlockSpec((GROUP, HEAD), lambda i, *_: (0, 0)),
            ],
            scratch_shapes=[pltpu.VMEM(kv.shape, jnp.float32)],
        ),
        out_shape=[
            jax.ShapeDtypeStruct((blocks, rows, width), jnp.bfloat16),
            jax.ShapeDtypeStruct(kv.shape, jnp.bfloat16),
            jax.ShapeDtypeStruct((GROUP, HEAD), jnp.float32),
        ],
        compiler_params=pltpu.CompilerParams(
            dimension_semantics=("arbitrary",), vmem_limit_bytes=48 * 1024 * 1024
        ),
        cost_estimate=pl.CostEstimate(
            flops=10 * blocks * GROUP * rows * 2 * BLOCK * HEAD,
            bytes_accessed=12 * 1024 * 1024,
            transcendentals=blocks * GROUP * rows * 2 * BLOCK,
        ),
    )(other, counts, own, kv, qg)


def split_kernel(k_ref, v_ref, out_ref):
    for n in range(out_ref.shape[0]):
        cols = slice(n * HEAD, (n + 1) * HEAD)
        out_ref[n, 0] = k_ref[:, cols]
        out_ref[n, 1] = v_ref[:, cols]


def split_heads(k, v, groups):
    return pl.pallas_call(
        split_kernel, out_shape=jax.ShapeDtypeStruct((groups, 2, BLOCK, HEAD), k.dtype)
    )(k, v)


def join_kernel(x_ref, dk_ref, dv_ref, dbq_ref):
    for n in range(x_ref.shape[0]):
        cols = slice(n * HEAD, (n + 1) * HEAD)
        dk_ref[:, cols] = x_ref[n, :BLOCK]
        dv_ref[:, cols] = x_ref[n, BLOCK : 2 * BLOCK]
        pieces = [
            x_ref[n, 2 * BLOCK + 16 * p : 2 * BLOCK + 16 * (p + 1)].astype(jnp.float32)
            for p in range(3)
        ]
        dbq_ref[n] = (pieces[0] + (pieces[1] + pieces[2]))[:GROUP]


def join_heads(x):
    groups = x.shape[0]
    flat = jax.ShapeDtypeStruct((BLOCK, groups * HEAD), jnp.bfloat16)
    return pl.pallas_call(
        join_kernel,
        out_shape=[flat, flat, jax.ShapeDtypeStruct((groups, GROUP, HEAD), jnp.float32)],
    )(x)


def pack_kernel(dkv_ref, dbq_ref, out_ref):
    rest = jnp.sum(dbq_ref[...], axis=0)
    pieces = []
    for _ in range(3):
        piece = rest.astype(jnp.bfloat16)
        rest = rest - piece.astype(jnp.float32)
        pieces.append(jnp.concatenate([piece, jnp.zeros_like(piece)], axis=0))
    for n in range(out_ref.shape[0]):
        out_ref[n, :BLOCK] = dkv_ref[n, 0]
        out_ref[n, BLOCK : 2 * BLOCK] = dkv_ref[n, 1]
        for p in range(3):
            out_ref[n, 2 * BLOCK + 16 * p : 2 * BLOCK + 16 * (p + 1)] = pieces[p]


def pack(dkv, dbq):
    return pl.pallas_call(
        pack_kernel,
        out_shape=jax.ShapeDtypeStruct((dkv.shape[0], 2 * BLOCK + 48, HEAD), jnp.bfloat16),
    )(dkv, dbq)


def by_group(x, groups):
    rows, width = x.shape
    return jnp.transpose(x.reshape(rows, groups, width // groups), (1, 0, 2))


def side_by_side(x):
    groups, rows, width = x.shape
    return jnp.transpose(x, (1, 0, 2)).reshape(rows, groups * width)


def body(q_lin, k_lin, value_projection, grad_out, q_bias, block_lists, block_counts):
    my_y = lax.axis_index("y")
    my_z = lax.axis_index("z")
    y_size = lax.axis_size("y")
    z_size = lax.axis_size("z")
    groups = y_size
    exchange = functools.partial(
        lax.all_to_all, axis_name="y", split_axis=0, concat_axis=0, tiled=True
    )

    kv_head = exchange(split_heads(k_lin[0], value_projection[0], groups))
    kv_all = lax.all_gather(kv_head, "z", axis=0, tiled=True)

    query_rows = (q_lin[0].astype(jnp.float32) + q_bias).astype(jnp.bfloat16)
    qg = jnp.stack([by_group(query_rows, groups), by_group(grad_out[0], groups)], axis=1)
    got = exchange(qg)

    mine = (GROUP, y_size, z_size)
    lists = lax.dynamic_slice_in_dim(block_lists[:, :, 1], my_y * GROUP, GROUP, axis=0)
    lists = lax.dynamic_index_in_dim(lists.reshape(mine), my_z, 2, keepdims=False)
    counts = lax.dynamic_slice_in_dim(block_counts, my_y * GROUP, GROUP, axis=0)
    counts = lax.dynamic_index_in_dim(counts.reshape(mine), my_z, 2, keepdims=False)
    other = lists % z_size * y_size + lists // z_size
    own = my_z * y_size + jnp.arange(y_size, dtype=jnp.int32)

    dq_head, dkv_all, dbq_part = attend(other, counts, own, kv_all, got)

    dkv_head = lax.psum_scatter(dkv_all, "z", scatter_dimension=0, tiled=True)
    dq_out = side_by_side(exchange(dq_head))[None]
    dbq_z = jnp.sum(lax.all_gather(dbq_part, "z", axis=0), axis=0)
    dbq_rep = lax.all_gather(dbq_z, REP, axis=0)
    dk_out, dv_out, dbq_out = join_heads(exchange(pack(dkv_head, dbq_rep)))
    dk_out, dv_out, dbq_out = dk_out[None], dv_out[None], dbq_out.reshape(-1)
    return dq_out, dk_out, dv_out, dbq_out


def solution(mesh):
    torus = Mesh(mesh.devices.reshape(4, 16, 4, 2), ("y", "z", "x", "core"))
    split = P(REP, SEQ, None)
    return jax.shard_map(
        body,
        mesh=torus,
        in_specs=(split, split, split, split, P(), P(), P()),
        out_specs=(split, split, split, P()),
        check_vma=False,
    )
```

time: 238 us -> 213 us (0.89)
  blocking collectives: 65.9 us -> 53.8 us
  waiting for transfers between devices: 112 us -> 103 us
  local copies, waits for them, and re-layouts: 13.9 us -> 10.1 us
    reduce_scatter x1, waiting for transfers between devices: 43.4 us -> 29.9 us  [body(): dkv_head = lax.psum_scatter(dkv_all, 'z', scatter_dimension=0, tiled=True)]
    all_gather x2 -> x1, blocking collectives: 25.8 us -> 13.6 us  [body(): dbq_rep = lax.all_gather(dbq_z, REP, axis=0)]
    pallas_call x1, Pallas kernels: 17.2 us -> 11.9 us  [attend(): pl.pallas_call(attend_kernel, grid_spec=pltpu.PrefetchScalarGridSpec(num_...]
    pallas_call x0 -> x3, Pallas kernels: none -> 5.12 us  [the longest x1 1.72 us: split_heads(): pl.pallas_call(split_kernel, out_shape=jax.ShapeDtypeStruct((groups, 2, B...]
    all_to_all x1, waiting for transfers between devices: 0.01 us -> 4.97 us  [body(): dk_out, dv_out, dbq_out = join_heads(exchange(pack(dkv_head, dbq_rep)))]
    optimization_barrier x1 -> x0, local copies, waits for them, and re-layouts: 2.71 us -> none  [body(): qg, kv_head = lax.optimization_barrier((qg, kv_head))]
    unnamed x18 -> x11, local copies, waits for them, and re-layouts: 6.95 us -> 6.23 us
  transfers between devices with their start and end apart: 5 -> 5, of which waited for: 3 -> 4; matrix products, arithmetic and copies ran while one was open for 4% -> 5% of each run, Pallas kernels for 0% -> 1%
where the time goes in v2:
time: 213 us; the launch traced here: 212 us
  waiting for transfers between devices  103 us (48%)
  blocking collectives  53.8 us (25%)
  Pallas kernels  17 us (8%)
  between operations  14.2 us (7%)
  starting transfers between devices  12.2 us (6%)
  local copies, waits for them, and re-layouts  10.1 us (5%)
    all_gather x1, waiting for transfers between devices, body(): kv_all = lax.all_gather(kv_head, 'z', axis=0, tiled=True)  43.9 us
    reduce_scatter x1, waiting for transfers between devices, body(): dkv_head = lax.psum_scatter(dkv_all, 'z', scatter_dimension=0, tiled=True)  29.9 us
    all_gather x1, blocking collectives, body(): dbq_z = jnp.sum(lax.all_gather(dbq_part, 'z', axis=0), axis=0)  29 us
    all_to_all x1, waiting for transfers between devices, body(): got = exchange(qg)  24.4 us
    all_gather x1, blocking collectives, body(): dbq_rep = lax.all_gather(dbq_z, REP, axis=0)  13.6 us
    pallas_call x1, Pallas kernels, attend(): pl.pallas_call(attend_kernel, grid_spec=pltpu.PrefetchScalarGridSpec(num_...  11.9 us
    all_to_all x1, blocking collectives, body(): kv_head = exchange(split_heads(k_lin[0], value_projection[0], groups))  11.2 us
    unnamed x11, local copies, waits for them, and re-layouts  6.23 us
  transfers between devices with their start and end apart: 5, of which 4 were waited for; matrix products, arithmetic and copies ran while one was open for 5% of the time, Pallas kernels for 1%

profile of v2, /device:TPU:2, one launch (start us, length us, event | category | flops | bytes accessed | tf_op | source)
XLA Modules:
  0.0 212.3 jit_solution(13007249870624283096)
XLA Ops:
  7.2 0.0 copy-start
  7.2 0.0 all-gather.4.cloned.1.call-start
  7.2 1.7 shard_map.102
  8.9 11.2 %all_to_all.20 = bf16[4,2,128,128]{3,2,1,0:T(8,128)(2,1)} all-to-all(bf16[4,2,128,128]{3,2,1,0:T(8,128)(2,1)} %shard_map.102), channel_id=1, replica_groups=mesh['y'=4,'z'=16,'x'=4,'core'=2] {'y'}, dimensions={0} | all-to-all | bytes 524288 | tf_op jit(solution)/shard_map/all_to_all | solution.py:208
  20.2 0.0 all-gather.4.cloned.1.call-update
  20.2 0.7 add.44
  20.9 1.6 copy.35
  22.6 0.5 copy.36
  23.1 1.6 copy.37
  24.7 1.3 copy.38
  26.0 0.0 copy-start.1
  26.0 0.3 fusion
  26.3 1.0 copy-done.1
  27.3 1.5 pad_maximum_fusion
  28.8 0.0 copy-start.3
  28.8 3.7 %all-to-all-start.1 = ((bf16[4,2,128,1024]{3,2,1,0:T(8,128)(2,1)}), bf16[4,2,128,1024]{3,2,1,0:T(8,128)(2,1)S(1)}, u32[]{:S(2)}, u32[]{:S(2)}) async-start(bf16[4,2,128,1024]{3,2,1,0:T(8,128)(2,1)} %pad_maximum_fusion), calls=%async_computation.1 | async-start | bytes 4194304 | tf_op jit(solution)/shard_map/all_to_all | solution.py:213
  32.5 0.0 reduce-scatter.2.cloned.1.call-start
  32.6 0.0 copy-done
  32.6 0.1 reshape.30
  32.7 0.0 copy-done.3
  32.7 0.1 reshape.29
  32.8 0.1 constant_dynamic-slice_fusion
  32.9 0.1 copy.34
  33.0 0.1 copy.39.count_ref
  33.1 0.1 copy.29
  33.2 0.1 copy.30
  33.3 24.4 %all-to-all-done.1.qg_ref = bf16[4,2,128,1024]{3,2,1,0:T(8,128)(2,1)S(1)} async-done(((bf16[4,2,128,1024]{3,2,1,0:T(8,128)(2,1)}), bf16[4,2,128,1024]{3,2,1,0:T(8,128)(2,1)S(1)}, u32[]{:S(2)}, u32[]{:S(2)}) %all-to-all-start.1) | async-done | bytes 2097184 | tf_op jit(solution)/shard_map/all_to_all | solution.py:213
  57.7 43.9 %all-gather.4.cloned.1.call-done.kv_ref = bf16[64,2,128,128]{3,2,1,0:T(8,128)(2,1)} async-done(((bf16[4,2,128,128]{3,2,1,0:T(8,128)(2,1)}), bf16[64,2,128,128]{3,2,1,0:T(8,128)(2,1)}) %all-gather.4.cloned.1.call-update) | async-done | bytes 4194320 | tf_op jit(solution)/shard_map/all_gather | solution.py:209
  101.6 11.9 %shard_map.103 = (bf16[4,128,1024]{2,1,0:T(8,128)(2,1)}, bf16[64,2,128,128]{3,2,1,0:T(8,128)(2,1)}, f32[8,128]{1,0:T(8,128)S(1)}) custom-call(s32[8,4]{1,0:T(8,128)S(1)} %fusion.2.other_ref, s32[8,4]{1,0:T(8,128)S(1)} %copy.39.count_ref, s32[4]{0:T(128)S(1)} %iota_add_fusion.own_ref, bf16[64,2,128,128]{3,2,1,0:T(8,128)(2,1)} %all-gather.4.cloned.1.call-done.kv_ref, ...), custom_call_target="tpu_custom_call" | custom-call | flops 1342177280 | bytes 12582912 | tf_op jit(solution)/shard_map/pallas_call | solution.py:104
  113.5 0.0 reduce-scatter.2.cloned.1.call-update
  113.5 4.3 %all-to-all-start.2 = ((bf16[4,128,1024]{2,1,0:T(8,128)(2,1)}), bf16[4,128,1024]{2,1,0:T(8,128)(2,1)S(1)}, u32[]{:S(2)}, u32[]{:S(2)}) async-start(bf16[4,128,1024]{2,1,0:T(8,128)(2,1)} %get-tuple-element.10), calls=%async_computation.2 | async-start | bytes 2097152 | tf_op jit(solution)/shard_map/all_to_all | solution.py:226
  117.9 29.0 %all-gather = f32[128,128]{1,0:T(8,128)S(1)} all-gather(f32[8,128]{1,0:T(8,128)S(1)} %get-tuple-element.12), channel_id=2, replica_groups=mesh['y'=4,'z'=16,'x'=4,'core'=2] {'z'}, dimensions={0}, use_global_device_ids=true | all-gather | bytes 69632 | tf_op jit(solution)/shard_map/all_gather | solution.py:227
  146.8 13.6 %all-gather.1 = f32[64,128]{1,0:T(8,128)} all-gather(f32[8,128]{1,0:T(8,128)S(1)} %bitcast_reduce_fusion), channel_id=3, replica_groups=mesh['y'=4,'z'=16,'x'=4,'core'=2] {'x','core'}, dimensions={0}, use_global_device_ids=true | all-gather | bytes 36864 | tf_op jit(solution)/shard_map/all_gather | solution.py:228
  160.4 29.9 %reduce-scatter.2.cloned.1.call-done.dkv_ref = bf16[4,2,128,128]{3,2,1,0:T(8,128)(2,1)} async-done(((bf16[64,2,128,128]{3,2,1,0:T(8,128)(2,1)}), bf16[4,2,128,128]{3,2,1,0:T(8,128)(2,1)}) %reduce-scatter.2.cloned.1.call-update) | async-done | bytes 262160 | tf_op jit(solution)/shard_map/reduce_scatter | solution.py:225
  190.3 1.7 shard_map.104
  192.0 0.0 all-to-all-done.2
  192.0 4.1 %all-to-all-start.3 = ((bf16[4,304,128]{2,1,0:T(8,128)(2,1)}), bf16[4,304,128]{2,1,0:T(8,128)(2,1)S(1)}, u32[]{:S(2)}, u32[]{:S(2)}) async-start(bf16[4,304,128]{2,1,0:T(8,128)(2,1)} %shard_map.104), calls=%async_computation.4 | async-start | bytes 622592 | tf_op jit(solution)/shard_map/all_to_all | solution.py:229
  196.1 0.7 copy.40
  196.8 1.3 copy.41
  198.1 5.0 %all-to-all-done.3.x_ref = bf16[4,304,128]{2,1,0:T(8,128)(2,1)S(1)} async-done(((bf16[4,304,128]{2,1,0:T(8,128)(2,1)}), bf16[4,304,128]{2,1,0:T(8,128)(2,1)S(1)}, u32[]{:S(2)}, u32[]{:S(2)}) %all-to-all-start.3) | async-done | bytes 311328 | tf_op jit(solution)/shard_map/all_to_all | solution.py:229
  203.0 0.0 copy-start.2
  203.0 0.7 copy-done.2
  203.8 1.7 shard_map.105
  (6 shorter events, 0.1 us)
Async XLA Ops:
  7.2 25.4 %copy-start = (s32[32,64]{1,0:T(8,128)S(1)}, s32[32,64]{1,0:T(8,128)}, u32[]{:S(2)}) copy-start(s32[32,64]{1,0:T(8,128)} %param.13) | copy-start | bytes 24580
  7.2 94.4 %all-gather.4.cloned.1.call-start = ((), (), s32[]{:S(2)}) async-start(), calls=%async_computation.5 | async-start | bytes 4456448 | tf_op jit(solution)/shard_map/all_gather | solution.py:209
  26.0 1.2 copy-start.1
  28.8 3.9 %copy-start.3 = (s32[32,64,2]{1,2,0:T(2,128)S(1)}, s32[32,64,2]{1,2,0:T(2,128)}, u32[]{:S(2)}) copy-start(s32[32,64,2]{1,2,0:T(2,128)} %param.12) | copy-start | bytes 49156
  28.8 28.9 %all-to-all-start.1 = ((bf16[4,2,128,1024]{3,2,1,0:T(8,128)(2,1)}), bf16[4,2,128,1024]{3,2,1,0:T(8,128)(2,1)S(1)}, u32[]{:S(2)}, u32[]{:S(2)}) async-start(bf16[4,2,128,1024]{3,2,1,0:T(8,128)(2,1)} %pad_maximum_fusion), calls=%async_computation.1 | async-start | bytes 4194304 | tf_op jit(solution)/shard_map/all_to_all | solution.py:213
  32.5 157.8 %reduce-scatter.2.cloned.1.call-start = ((), (), s32[]{:S(2)}) async-start(), calls=%async_computation.6 | async-start | bytes 4456448 | tf_op jit(solution)/shard_map/reduce_scatter | solution.py:225
  113.5 78.5 %all-to-all-start.2 = ((bf16[4,128,1024]{2,1,0:T(8,128)(2,1)}), bf16[4,128,1024]{2,1,0:T(8,128)(2,1)S(1)}, u32[]{:S(2)}, u32[]{:S(2)}) async-start(bf16[4,128,1024]{2,1,0:T(8,128)(2,1)} %get-tuple-element.10), calls=%async_computation.2 | async-start | bytes 2097152 | tf_op jit(solution)/shard_map/all_to_all | solution.py:226
  192.0 11.0 %all-to-all-start.3 = ((bf16[4,304,128]{2,1,0:T(8,128)(2,1)}), bf16[4,304,128]{2,1,0:T(8,128)(2,1)S(1)}, u32[]{:S(2)}, u32[]{:S(2)}) async-start(bf16[4,304,128]{2,1,0:T(8,128)(2,1)} %shard_map.104), calls=%async_computation.4 | async-start | bytes 622592 | tf_op jit(solution)/shard_map/all_to_all | solution.py:229
  203.0 0.7 copy-start.2
Sparse Core Ops, SparseCore 0:
  20.3 81.2 all-gather.3
  113.7 76.6 reduce-scatter.1

commit v3 on v2

--- a/solution.py
+++ b/solution.py
@@ -14,6 +14,8 @@
 BLOCK = 128
 GROUP = 8
 NEG = -1e30
+CHUNKS = 4
+SMALL = pltpu.CompilerParams(vmem_limit_bytes=8 * 1024 * 1024)
 
 
 def dot(a, b, ca, cb):
@@ -21,15 +23,26 @@
 
 
 def attend_kernel(
-    other_ref, count_ref, own_ref, kv_ref, qg_ref, dq_ref, dkv_ref, dbq_ref, acc_ref
+    other_ref, count_ref, own_ref, kv_hbm, qg_ref, dq_ref, dkv_hbm, dbq_ref, kv_ref, acc_ref, sems
 ):
     step = pl.program_id(0)
     scaling = HEAD**-0.5
+    tiles = kv_ref.shape[0]
+    chunk = tiles // CHUNKS
+    parts = [pl.ds(n * chunk, chunk) for n in range(CHUNKS)]
 
     @pl.when(step == 0)
     def _():
+        loads = [
+            pltpu.make_async_copy(kv_hbm.at[part], kv_ref.at[part], sems.at[n])
+            for n, part in enumerate(parts)
+        ]
+        for load in loads:
+            load.start()
         acc_ref[...] = jnp.zeros_like(acc_ref)
         dbq_ref[...] = jnp.zeros_like(dbq_ref)
+        for load in loads:
+            load.wait()
 
     heads = range(GROUP)
     cols = [slice(h * HEAD, (h + 1) * HEAD) for h in heads]
@@ -92,27 +105,42 @@
 
     @pl.when(step == pl.num_programs(0) - 1)
     def _():
-        @pl.loop(0, acc_ref.shape[0])
-        def _(n):
-            dkv_ref[n, 0] = (acc_ref[n, 0] * scaling).astype(jnp.bfloat16)
-            dkv_ref[n, 1] = acc_ref[n, 1].astype(jnp.bfloat16)
+        stores = []
+        for n, part in enumerate(parts):
+
+            @pl.loop(n * chunk, (n + 1) * chunk)
+            def _(tile):
+                kv_ref[tile, 0] = (acc_ref[tile, 0] * scaling).astype(jnp.bfloat16)
+                kv_ref[tile, 1] = acc_ref[tile, 1].astype(jnp.bfloat16)
+
+            store = pltpu.make_async_copy(kv_ref.at[part], dkv_hbm.at[part], sems.at[n])
+            store.start()
+            stores.append(store)
+        for store in stores:
+            store.wait()
 
 
 def attend(other, counts, own, kv, qg):
     blocks, _, rows, width = qg.shape
-    whole = pl.BlockSpec(kv.shape, lambda i, *_: (0, 0, 0, 0))
     return pl.pallas_call(
         attend_kernel,
         grid_spec=pltpu.PrefetchScalarGridSpec(
             num_scalar_prefetch=3,
             grid=(blocks,),
-            in_specs=[whole, pl.BlockSpec((1, 2, rows, width), lambda i, *_: (i, 0, 0, 0))],
+            in_specs=[
+                pl.BlockSpec(memory_space=pl.ANY),
+                pl.BlockSpec((1, 2, rows, width), lambda i, *_: (i, 0, 0, 0)),
+            ],
             out_specs=[
                 pl.BlockSpec((1, rows, width), lambda i, *_: (i, 0, 0)),
-                whole,
+                pl.BlockSpec(memory_space=pl.ANY),
                 pl.BlockSpec((GROUP, HEAD), lambda i, *_: (0, 0)),
             ],
-            scratch_shapes=[pltpu.VMEM(kv.shape, jnp.float32)],
+            scratch_shapes=[
+                pltpu.VMEM(kv.shape, jnp.bfloat16),
+                pltpu.VMEM(kv.shape, jnp.float32),
+                pltpu.SemaphoreType.DMA((CHUNKS,)),
+            ],
         ),
         out_shape=[
             jax.ShapeDtypeStruct((blocks, rows, width), jnp.bfloat16),
@@ -120,7 +148,7 @@
             jax.ShapeDtypeStruct((GROUP, HEAD), jnp.float32),
         ],
         compiler_params=pltpu.CompilerParams(
-            dimension_semantics=("arbitrary",), vmem_limit_bytes=48 * 1024 * 1024
+            dimension_semantics=("arbitrary",), vmem_limit_bytes=60 * 1024 * 1024
         ),
         cost_estimate=pl.CostEstimate(
             flops=10 * blocks * GROUP * rows * 2 * BLOCK * HEAD,
@@ -139,11 +167,16 @@
 
 def split_heads(k, v, groups):
     return pl.pallas_call(
-        split_kernel, out_shape=jax.ShapeDtypeStruct((groups, 2, BLOCK, HEAD), k.dtype)
+        split_kernel,
+        compiler_params=SMALL,
+        out_shape=jax.ShapeDtypeStruct((groups, 2, BLOCK, HEAD), k.dtype),
     )(k, v)
 
 
-def join_kernel(x_ref, dk_ref, dv_ref, dbq_ref):
+def join_kernel(x_any, dk_ref, dv_ref, dbq_ref, x_ref, sem):
+    load = pltpu.make_async_copy(x_any, x_ref, sem)
+    load.start()
+    load.wait()
     for n in range(x_ref.shape[0]):
         cols = slice(n * HEAD, (n + 1) * HEAD)
         dk_ref[:, cols] = x_ref[n, :BLOCK]
@@ -160,6 +193,9 @@
     flat = jax.ShapeDtypeStruct((BLOCK, groups * HEAD), jnp.bfloat16)
     return pl.pallas_call(
         join_kernel,
+        compiler_params=SMALL,
+        in_specs=[pl.BlockSpec(memory_space=pl.ANY)],
+        scratch_shapes=[pltpu.VMEM(x.shape, x.dtype), pltpu.SemaphoreType.DMA],
         out_shape=[flat, flat, jax.ShapeDtypeStruct((groups, GROUP, HEAD), jnp.float32)],
     )(x)
 
@@ -181,6 +217,7 @@
 def pack(dkv, dbq):
     return pl.pallas_call(
         pack_kernel,
+        compiler_params=SMALL,
         out_shape=jax.ShapeDtypeStruct((dkv.shape[0], 2 * BLOCK + 48, HEAD), jnp.bfloat16),
     )(dkv, dbq)
 

time: 213 us -> 212 us (level)
  local copies, waits for them, and re-layouts: 10.1 us -> 12.8 us
  Pallas kernels: 17 us -> 14.3 us
    pallas_call x3, Pallas kernels: 5.12 us -> 1.61 us  [the longest x1 0.83 us: join_heads(): pl.pallas_call(join_kernel, compiler_params=SMALL, in_specs=[pl.BlockSpec...]
    unnamed x11 -> x19, local copies, waits for them, and re-layouts: 6.23 us -> 8.28 us
  transfers between devices with their start and end apart: 5 -> 5, of which waited for: 4 -> 4; matrix products, arithmetic and copies ran while one was open for 5% -> 6% of each run, Pallas kernels for 1% -> 0%
where the time goes in v3:
time: 212 us; the launch traced here: 211 us
  waiting for transfers between devices  102 us (48%)
  blocking collectives  52.8 us (25%)
  Pallas kernels  14.3 us (7%)
  between operations  14.2 us (7%)
  local copies, waits for them, and re-layouts  12.8 us (6%)
  starting transfers between devices  12.2 us (6%)
  other arithmetic  2.92 us (1%)
    all_gather x1, waiting for transfers between devices, body(): kv_all = lax.all_gather(kv_head, 'z', axis=0, tiled=True)  43.8 us
    reduce_scatter x1, waiting for transfers between devices, body(): dkv_head = lax.psum_scatter(dkv_all, 'z', scatter_dimension=0, tiled=True)  30.6 us
    all_gather x1, blocking collectives, body(): dbq_z = jnp.sum(lax.all_gather(dbq_part, 'z', axis=0), axis=0)  29 us
    all_to_all x1, waiting for transfers between devices, body(): got = exchange(qg)  22.7 us
    all_gather x1, blocking collectives, body(): dbq_rep = lax.all_gather(dbq_z, REP, axis=0)  12.8 us
    pallas_call x1, Pallas kernels, attend(): pl.pallas_call(attend_kernel, grid_spec=pltpu.PrefetchScalarGridSpec(num_...  12.6 us
    all_to_all x1, blocking collectives, body(): kv_head = exchange(split_heads(k_lin[0], value_projection[0], groups))  11 us
    unnamed x19, local copies, waits for them, and re-layouts  8.28 us
  transfers between devices with their start and end apart: 5, of which 4 were waited for; matrix products, arithmetic and copies ran while one was open for 6% of the time, Pallas kernels for 0%

profile of v3, /device:TPU:2, one launch (start us, length us, event | category | flops | bytes accessed | tf_op | source)
XLA Modules:
  0.0 211.3 jit_solution(10906360902002845331)
XLA Ops:
  7.2 0.0 copy-start
  7.2 0.0 all-gather.4.cloned.1.call-start
  7.2 0.0 copy-start.2
  7.2 0.9 copy-done.2
  8.1 0.0 copy-start.3
  8.1 0.9 copy-done.3
  9.1 11.0 %all_to_all.20 = bf16[4,2,128,128]{3,2,1,0:T(8,128)(2,1)} all-to-all(bf16[4,2,128,128]{3,2,1,0:T(8,128)(2,1)S(1)} %shard_map.102), channel_id=1, replica_groups=mesh['y'=4,'z'=16,'x'=4,'core'=2] {'y'}, dimensions={0} | all-to-all | bytes 524288 | tf_op jit(solution)/shard_map/all_to_all | solution.py:245
  20.1 0.0 all-gather.4.cloned.1.call-update
  20.2 0.7 add.44
  20.9 1.6 copy.35
  22.5 0.5 copy.36
  23.0 1.6 copy.37
  24.7 1.3 copy.38
  26.0 0.3 fusion
  26.3 1.0 copy-done.5
  27.2 1.5 pad_maximum_fusion
  28.7 3.7 %all-to-all-start.1 = ((bf16[4,2,128,1024]{3,2,1,0:T(8,128)(2,1)}), bf16[4,2,128,1024]{3,2,1,0:T(8,128)(2,1)S(1)}, u32[]{:S(2)}, u32[]{:S(2)}) async-start(bf16[4,2,128,1024]{3,2,1,0:T(8,128)(2,1)} %pad_maximum_fusion), calls=%async_computation.1 | async-start | bytes 4194304 | tf_op jit(solution)/shard_map/all_to_all | solution.py:250
  32.5 0.0 reduce-scatter.2.cloned.1.call-start
  32.5 0.0 copy-done
  32.6 0.1 reshape.30
  32.6 0.0 copy-done.6
  32.7 0.1 reshape.29
  32.8 0.1 constant_dynamic-slice_fusion
  32.9 0.1 copy.34
  33.0 0.7 copy.39.count_ref
  33.7 0.1 copy.29
  33.8 0.1 copy.30
  33.8 0.5 iota_add_fusion.own_ref
  34.4 0.6 fusion.2.other_ref
  35.0 22.7 %all-to-all-done.1.qg_ref = bf16[4,2,128,1024]{3,2,1,0:T(8,128)(2,1)S(1)} async-done(((bf16[4,2,128,1024]{3,2,1,0:T(8,128)(2,1)}), bf16[4,2,128,1024]{3,2,1,0:T(8,128)(2,1)S(1)}, u32[]{:S(2)}, u32[]{:S(2)}) %all-to-all-start.1) | async-done | bytes 2097184 | tf_op jit(solution)/shard_map/all_to_all | solution.py:250
  57.7 43.8 %all-gather.4.cloned.1.call-done.kv_hbm = bf16[64,2,128,128]{3,2,1,0:T(8,128)(2,1)} async-done(((bf16[4,2,128,128]{3,2,1,0:T(8,128)(2,1)}), bf16[64,2,128,128]{3,2,1,0:T(8,128)(2,1)}) %all-gather.4.cloned.1.call-update) | async-done | bytes 4194320 | tf_op jit(solution)/shard_map/all_gather | solution.py:246
  101.5 0.0 copy-done.4
  101.5 12.6 %shard_map.103 = (bf16[4,128,1024]{2,1,0:T(8,128)(2,1)}, bf16[64,2,128,128]{3,2,1,0:T(8,128)(2,1)}, f32[8,128]{1,0:T(8,128)}) custom-call(s32[8,4]{1,0:T(8,128)} %fusion.2.other_ref, s32[8,4]{1,0:T(8,128)} %copy.39.count_ref, s32[4]{0:T(128)} %iota_add_fusion.own_ref, bf16[64,2,128,128]{3,2,1,0:T(8,128)(2,1)} %all-gather.4.cloned.1.call-done.kv_hbm, ...), custom_call_target="tpu_custom_call" | custom-call | flops 1342177280 | bytes 12582912 | tf_op jit(solution)/shard_map/pallas_call | solution.py:125
  114.2 0.0 reduce-scatter.2.cloned.1.call-update
  114.2 0.0 copy-start.7
  114.2 4.3 %all-to-all-start.2 = ((bf16[4,128,1024]{2,1,0:T(8,128)(2,1)}), bf16[4,128,1024]{2,1,0:T(8,128)(2,1)S(1)}, u32[]{:S(2)}, u32[]{:S(2)}) async-start(bf16[4,128,1024]{2,1,0:T(8,128)(2,1)} %get-tuple-element.10), calls=%async_computation.2 | async-start | bytes 2097152 | tf_op jit(solution)/shard_map/all_to_all | solution.py:263
  118.5 0.0 copy-done.7
  118.5 29.0 %all-gather = f32[128,128]{1,0:T(8,128)S(1)} all-gather(f32[8,128]{1,0:T(8,128)S(1)} %copy-done.7), channel_id=2, replica_groups=mesh['y'=4,'z'=16,'x'=4,'core'=2] {'z'}, dimensions={0}, use_global_device_ids=true | all-gather | bytes 69632 | tf_op jit(solution)/shard_map/all_gather | solution.py:264
  147.5 12.8 %all-gather.1 = f32[64,128]{1,0:T(8,128)S(1)} all-gather(f32[8,128]{1,0:T(8,128)S(1)} %bitcast_reduce_fusion), channel_id=3, replica_groups=mesh['y'=4,'z'=16,'x'=4,'core'=2] {'x','core'}, dimensions={0}, use_global_device_ids=true | all-gather | bytes 36864 | tf_op jit(solution)/shard_map/all_gather | solution.py:265
  160.3 30.6 %reduce-scatter.2.cloned.1.call-done.dkv_ref = bf16[4,2,128,128]{3,2,1,0:T(8,128)(2,1)} async-done(((bf16[64,2,128,128]{3,2,1,0:T(8,128)(2,1)}), bf16[4,2,128,128]{3,2,1,0:T(8,128)(2,1)}) %reduce-scatter.2.cloned.1.call-update) | async-done | bytes 262160 | tf_op jit(solution)/shard_map/reduce_scatter | solution.py:262
  190.8 0.9 copy-done.1
  191.8 0.7 shard_map.104
  192.5 0.0 all-to-all-done.2
  192.5 4.1 %all-to-all-start.3 = ((bf16[4,304,128]{2,1,0:T(8,128)(2,1)}), bf16[4,304,128]{2,1,0:T(8,128)(2,1)S(1)}, u32[]{:S(2)}, u32[]{:S(2)}) async-start(bf16[4,304,128]{2,1,0:T(8,128)(2,1)} %shard_map.104), calls=%async_computation.4 | async-start | bytes 622592 | tf_op jit(solution)/shard_map/all_to_all | solution.py:266
  196.7 0.7 copy.40
  197.3 1.3 copy.41
  198.6 5.0 %all-to-all-done.3.x_any = bf16[4,304,128]{2,1,0:T(8,128)(2,1)S(1)} async-done(((bf16[4,304,128]{2,1,0:T(8,128)(2,1)}), bf16[4,304,128]{2,1,0:T(8,128)(2,1)S(1)}, u32[]{:S(2)}, u32[]{:S(2)}) %all-to-all-start.3) | async-done | bytes 311328 | tf_op jit(solution)/shard_map/all_to_all | solution.py:266
  203.6 0.8 shard_map.105
  (9 shorter events, 0.1 us)
Async XLA Ops:
  7.2 25.4 %copy-start = (s32[32,64]{1,0:T(8,128)S(1)}, s32[32,64]{1,0:T(8,128)}, u32[]{:S(2)}) copy-start(s32[32,64]{1,0:T(8,128)} %param.13) | copy-start | bytes 24580
  7.2 94.3 %all-gather.4.cloned.1.call-start = ((), (), s32[]{:S(2)}) async-start(), calls=%async_computation.5 | async-start | bytes 4456448 | tf_op jit(solution)/shard_map/all_gather | solution.py:246
  7.2 0.9 copy-start.2
  8.1 0.9 copy-start.3
  26.0 1.2 copy-start.5
  28.7 3.9 %copy-start.6 = (s32[32,64,2]{1,2,0:T(2,128)S(1)}, s32[32,64,2]{1,2,0:T(2,128)}, u32[]{:S(2)}) copy-start(s32[32,64,2]{1,2,0:T(2,128)} %param.12) | copy-start | bytes 49156
  28.7 28.9 %all-to-all-start.1 = ((bf16[4,2,128,1024]{3,2,1,0:T(8,128)(2,1)}), bf16[4,2,128,1024]{3,2,1,0:T(8,128)(2,1)S(1)}, u32[]{:S(2)}, u32[]{:S(2)}) async-start(bf16[4,2,128,1024]{3,2,1,0:T(8,128)(2,1)} %pad_maximum_fusion), calls=%async_computation.1 | async-start | bytes 4194304 | tf_op jit(solution)/shard_map/all_to_all | solution.py:250
  32.5 158.3 %reduce-scatter.2.cloned.1.call-start = ((), (), s32[]{:S(2)}) async-start(), calls=%async_computation.6 | async-start | bytes 4456448 | tf_op jit(solution)/shard_map/reduce_scatter | solution.py:262
  57.7 43.9 %copy-start.4 = (bf16[4,2,128,1024]{3,2,1,0:T(8,128)(2,1)}, bf16[4,2,128,1024]{3,2,1,0:T(8,128)(2,1)S(1)}, u32[]{:S(2)}) copy-start(bf16[4,2,128,1024]{3,2,1,0:T(8,128)(2,1)S(1)} %all-to-all-done.1.qg_ref) | copy-start | bytes 6291460
  114.2 4.3 %copy-start.7 = (f32[8,128]{1,0:T(8,128)S(1)}, f32[8,128]{1,0:T(8,128)}, u32[]{:S(2)}) copy-start(f32[8,128]{1,0:T(8,128)} %get-tuple-element.12) | copy-start | bytes 12292
  114.2 78.3 %all-to-all-start.2 = ((bf16[4,128,1024]{2,1,0:T(8,128)(2,1)}), bf16[4,128,1024]{2,1,0:T(8,128)(2,1)S(1)}, u32[]{:S(2)}, u32[]{:S(2)}) async-start(bf16[4,128,1024]{2,1,0:T(8,128)(2,1)} %get-tuple-element.10), calls=%async_computation.2 | async-start | bytes 2097152 | tf_op jit(solution)/shard_map/all_to_all | solution.py:263
  190.8 0.9 copy-start.1
  192.5 11.1 %all-to-all-start.3 = ((bf16[4,304,128]{2,1,0:T(8,128)(2,1)}), bf16[4,304,128]{2,1,0:T(8,128)(2,1)S(1)}, u32[]{:S(2)}, u32[]{:S(2)}) async-start(bf16[4,304,128]{2,1,0:T(8,128)(2,1)} %shard_map.104), calls=%async_computation.4 | async-start | bytes 622592 | tf_op jit(solution)/shard_map/all_to_all | solution.py:266
Sparse Core Ops, SparseCore 0:
  20.3 81.1 all-gather.3
  114.3 76.4 reduce-scatter.1

commit v4 on v3

v4 whole, which is shorter than its diff:
```python
import functools

import jax
import jax.numpy as jnp
from jax import lax
from jax.experimental import pallas as pl
from jax.experimental.pallas import tpu as pltpu
from jax.sharding import Mesh
from jax.sharding import PartitionSpec as P

SEQ = ("y", "z")
REP = ("x", "core")
HEAD = 128
BLOCK = 128
GROUP = 8
NEG = -1e30
SCALING = HEAD**-0.5
COLS = [slice(h * HEAD, (h + 1) * HEAD) for h in range(GROUP)]
CHUNKS = 4
SMALL = pltpu.CompilerParams(vmem_limit_bytes=8 * 1024 * 1024)


def dot(a, b, ca, cb):
    return lax.dot_general(a, b, (((ca,), (cb,)), ((), ())), preferred_element_type=jnp.float32)


def side(parts):
    return jnp.concatenate(parts, axis=1)


def own_kernel(kv_ref, qg_ref, raised_ref, wg_ref, stats_ref):
    q_all = jnp.concatenate([qg_ref[0, 0, :, c] for c in COLS], axis=0)
    g_all = jnp.concatenate([qg_ref[0, 1, :, c] for c in COLS], axis=0)
    scores = dot(kv_ref[0, 0], q_all, 1, 1)
    top = jnp.max(scores, axis=0, keepdims=True)
    raised = jnp.exp((scores - top) * SCALING)
    raised_ref[0] = raised
    wg_ref[0] = dot(kv_ref[0, 1], g_all, 1, 1)
    stats_ref[0] = jnp.zeros_like(stats_ref[0])
    stats_ref[0, 0:1, :] = top
    stats_ref[0, 1:2, :] = jnp.sum(raised, axis=0, keepdims=True)


def own_part(kv_head, qg):
    blocks, _, rows, width = qg.shape
    square = pl.BlockSpec((1, BLOCK, width), lambda i: (i, 0, 0))
    return pl.pallas_call(
        own_kernel,
        grid=(blocks,),
        in_specs=[
            pl.BlockSpec((1, 2, BLOCK, HEAD), lambda i: (i, 0, 0, 0)),
            pl.BlockSpec((1, 2, rows, width), lambda i: (i, 0, 0, 0)),
        ],
        out_specs=[square, square, pl.BlockSpec((1, 8, width), lambda i: (i, 0, 0))],
        out_shape=[
            jax.ShapeDtypeStruct((blocks, BLOCK, width), jnp.float32),
            jax.ShapeDtypeStruct((blocks, BLOCK, width), jnp.float32),
            jax.ShapeDtypeStruct((blocks, 8, width), jnp.float32),
        ],
        compiler_params=pltpu.CompilerParams(vmem_limit_bytes=32 * 1024 * 1024),
        cost_estimate=pl.CostEstimate(
            flops=4 * blocks * BLOCK * width * HEAD,
            bytes_accessed=7 * 1024 * 1024,
            transcendentals=blocks * BLOCK * width,
        ),
    )(kv_head, qg)


def key_kernel(
    other_ref,
    count_ref,
    own_ref,
    kv_hbm,
    qg_ref,
    raised_ref,
    wg_ref,
    stats_ref,
    dkv_hbm,
    sg_ref,
    kv_ref,
    acc_ref,
    sems,
):
    step = pl.program_id(0)
    chunk = kv_ref.shape[0] // CHUNKS
    parts = [pl.ds(n * chunk, chunk) for n in range(CHUNKS)]

    @pl.when(step == 0)
    def _():
        loads = [
            pltpu.make_async_copy(kv_hbm.at[part], kv_ref.at[part], sems.at[n])
            for n, part in enumerate(parts)
        ]
        for load in loads:
            load.start()
        acc_ref[...] = jnp.zeros_like(acc_ref)
        for load in loads:
            load.wait()

    heads = range(GROUP)
    own = own_ref[step]
    others = [other_ref[h, step] for h in heads]
    q = [qg_ref[0, 0, :, c] for c in COLS]
    g = [qg_ref[0, 1, :, c] for c in COLS]
    closed = side(
        [jnp.full((1, BLOCK), jnp.where(count_ref[h, step] > 1, 0.0, NEG)) for h in heads]
    )
    scores = side([dot(kv_ref[others[h], 0], q[h], 1, 1) for h in heads]) + closed
    wg_other = side([dot(kv_ref[others[h], 1], g[h], 1, 1) for h in heads])
    top_own = stats_ref[0, 0:1, :]
    top = jnp.maximum(top_own, jnp.max(scores, axis=0, keepdims=True))
    raised = jnp.exp((scores - top) * SCALING)
    lower = jnp.exp((top_own - top) * SCALING)
    share = 1.0 / (stats_ref[0, 1:2, :] * lower + jnp.sum(raised, axis=0, keepdims=True))
    weights_own = raised_ref[0] * (lower * share)
    weights_other = raised * share
    half_own = weights_own.astype(jnp.bfloat16)
    half_other = weights_other.astype(jnp.bfloat16)
    wg_own = wg_ref[0]
    row_dots = jnp.sum(
        half_own.astype(jnp.float32) * wg_own + half_other.astype(jnp.float32) * wg_other,
        axis=0,
        keepdims=True,
    )
    sg_own = (weights_own * (wg_own - row_dots)).astype(jnp.bfloat16)
    sg_other = (weights_other * (wg_other - row_dots)).astype(jnp.bfloat16)
    sg_ref[0, 0] = sg_own
    sg_ref[0, 1] = sg_other
    dk_own = dot(sg_own, jnp.concatenate(q, axis=0), 1, 0)
    dv_own = dot(half_own, jnp.concatenate(g, axis=0), 1, 0)
    dk_other = [dot(sg_other[:, COLS[h]], q[h], 1, 0) for h in heads]
    dv_other = [dot(half_other[:, COLS[h]], g[h], 1, 0) for h in heads]
    acc_ref[own, 0] += dk_own
    acc_ref[own, 1] += dv_own
    for h in heads:
        acc_ref[others[h], 0] += dk_other[h]
        acc_ref[others[h], 1] += dv_other[h]

    @pl.when(step == pl.num_programs(0) - 1)
    def _():
        stores = []
        for n, part in enumerate(parts):

            @pl.loop(n * chunk, (n + 1) * chunk)
            def _(tile):
                kv_ref[tile, 0] = (acc_ref[tile, 0] * SCALING).astype(jnp.bfloat16)
                kv_ref[tile, 1] = acc_ref[tile, 1].astype(jnp.bfloat16)

            store = pltpu.make_async_copy(kv_ref.at[part], dkv_hbm.at[part], sems.at[n])
            store.start()
            stores.append(store)
        for store in stores:
            store.wait()


def key_part(other, counts, own, kv, qg, raised, wg, stats):
    blocks, _, rows, width = qg.shape
    square = pl.BlockSpec((1, BLOCK, width), lambda i, *_: (i, 0, 0))
    double = pl.BlockSpec((1, 2, BLOCK, width), lambda i, *_: (i, 0, 0, 0))
    return pl.pallas_call(
        key_kernel,
        grid_spec=pltpu.PrefetchScalarGridSpec(
            num_scalar_prefetch=3,
            grid=(blocks,),
            in_specs=[
                pl.BlockSpec(memory_space=pl.ANY),
                double,
                square,
                square,
                pl.BlockSpec((1, 8, width), lambda i, *_: (i, 0, 0)),
            ],
            out_specs=[pl.BlockSpec(memory_space=pl.ANY), double],
            scratch_shapes=[
                pltpu.VMEM(kv.shape, jnp.bfloat16),
                pltpu.VMEM(kv.shape, jnp.float32),
                pltpu.SemaphoreType.DMA((CHUNKS,)),
            ],
        ),
        out_shape=[
            jax.ShapeDtypeStruct(kv.shape, jnp.bfloat16),
            jax.ShapeDtypeStruct((blocks, 2, BLOCK, width), jnp.bfloat16),
        ],
        compiler_params=pltpu.CompilerParams(
            dimension_semantics=("arbitrary",), vmem_limit_bytes=60 * 1024 * 1024
        ),
        cost_estimate=pl.CostEstimate(
            flops=12 * blocks * BLOCK * width * HEAD,
            bytes_accessed=16 * 1024 * 1024,
            transcendentals=blocks * BLOCK * width,
        ),
    )(other, counts, own, kv, qg, raised, wg, stats)


def query_kernel(other_ref, kv_ref, own_ref, sg_ref, dq_ref, dbq_ref):
    step = pl.program_id(0)

    @pl.when(step == 0)
    def _():
        dbq_ref[...] = jnp.zeros_like(dbq_ref)

    sums = []
    for h in range(GROUP):
        grads = jnp.concatenate([sg_ref[0, 0, :, COLS[h]], sg_ref[0, 1, :, COLS[h]]], axis=0)
        keys = jnp.concatenate([own_ref[0, 0], kv_ref[other_ref[h, step], 0]], axis=0)
        grad_q = SCALING * dot(grads, keys, 0, 0)
        dq_ref[0, :, COLS[h]] = grad_q.astype(jnp.bfloat16)
        sums.append(jnp.sum(grad_q, axis=0, keepdims=True))
    dbq_ref[...] += jnp.concatenate(sums, axis=0)


def query_part(other, kv, kv_head, sg):
    blocks, _, rows, width = sg.shape
    return pl.pallas_call(
        query_kernel,
        grid_spec=pltpu.PrefetchScalarGridSpec(
            num_scalar_prefetch=1,
            grid=(blocks,),
            in_specs=[
                pl.BlockSpec(kv.shape, lambda i, *_: (0, 0, 0, 0)),
                pl.BlockSpec((1, 2, BLOCK, HEAD), lambda i, *_: (i, 0, 0, 0)),
                pl.BlockSpec((1, 2, BLOCK, width), lambda i, *_: (i, 0, 0, 0)),
            ],
            out_specs=[
                pl.BlockSpec((1, rows, width), lambda i, *_: (i, 0, 0)),
                pl.BlockSpec((GROUP, HEAD), lambda i, *_: (0, 0)),
            ],
        ),
        out_shape=[
            jax.ShapeDtypeStruct((blocks, rows, width), jnp.bfloat16),
            jax.ShapeDtypeStruct((GROUP, HEAD), jnp.float32),
        ],
        compiler_params=pltpu.CompilerParams(
            dimension_semantics=("arbitrary",), vmem_limit_bytes=32 * 1024 * 1024
        ),
        cost_estimate=pl.CostEstimate(
            flops=4 * blocks * BLOCK * width * HEAD,
            bytes_accessed=7 * 1024 * 1024,
            transcendentals=0,
        ),
    )(other, kv, kv_head, sg)


def split_kernel(k_ref, v_ref, out_ref):
    for n in range(out_ref.shape[0]):
        cols = slice(n * HEAD, (n + 1) * HEAD)
        out_ref[n, 0] = k_ref[:, cols]
        out_ref[n, 1] = v_ref[:, cols]


def split_heads(k, v, groups):
    return pl.pallas_call(
        split_kernel,
        compiler_params=SMALL,
        out_shape=jax.ShapeDtypeStruct((groups, 2, BLOCK, HEAD), k.dtype),
    )(k, v)


def join_kernel(x_any, dk_ref, dv_ref, x_ref, sem):
    load = pltpu.make_async_copy(x_any, x_ref, sem)
    load.start()
    load.wait()
    for n in range(x_ref.shape[0]):
        cols = slice(n * HEAD, (n + 1) * HEAD)
        dk_ref[:, cols] = x_ref[n, 0]
        dv_ref[:, cols] = x_ref[n, 1]


def join_heads(x):
    flat = jax.ShapeDtypeStruct((BLOCK, x.shape[0] * HEAD), jnp.bfloat16)
    return pl.pallas_call(
        join_kernel,
        compiler_params=SMALL,
        in_specs=[pl.BlockSpec(memory_space=pl.ANY)],
        scratch_shapes=[pltpu.VMEM(x.shape, x.dtype), pltpu.SemaphoreType.DMA],
        out_shape=[flat, flat],
    )(x)


def pieces_kernel(dbq_ref, out_ref):
    rest = jnp.sum(dbq_ref[...], axis=0)
    row = lax.broadcasted_iota(jnp.int32, (16, HEAD), 0)
    blocks = [jnp.zeros((16, HEAD), jnp.float32)] * GROUP
    for p in range(3):
        piece = rest.astype(jnp.bfloat16).astype(jnp.float32)
        rest = rest - piece
        blocks = [jnp.where(row == p, piece[h : h + 1], blocks[h]) for h in range(GROUP)]
    for h in range(GROUP):
        out_ref[:, COLS[h]] = blocks[h].astype(jnp.bfloat16)


def pieces(dbq):
    return pl.pallas_call(
        pieces_kernel,
        compiler_params=SMALL,
        out_shape=jax.ShapeDtypeStruct((16, GROUP * HEAD), jnp.bfloat16),
    )(dbq)


def by_group(x, groups):
    rows, width = x.shape
    return jnp.transpose(x.reshape(rows, groups, width // groups), (1, 0, 2))


def side_by_side(x):
    groups, rows, width = x.shape
    return jnp.transpose(x, (1, 0, 2)).reshape(rows, groups * width)


def body(q_lin, k_lin, value_projection, grad_out, q_bias, block_lists, block_counts):
    my_y = lax.axis_index("y")
    my_z = lax.axis_index("z")
    y_size = lax.axis_size("y")
    z_size = lax.axis_size("z")
    groups = y_size
    exchange = functools.partial(
        lax.all_to_all, axis_name="y", split_axis=0, concat_axis=0, tiled=True
    )

    kv_head = exchange(split_heads(k_lin[0], value_projection[0], groups))
    kv_all = lax.all_gather(kv_head, "z", axis=0, tiled=True)

    query_rows = (q_lin[0].astype(jnp.float32) + q_bias).astype(jnp.bfloat16)
    qg = jnp.stack([by_group(query_rows, groups), by_group(grad_out[0], groups)], axis=1)
    got = exchange(qg)

    mine = (GROUP, y_size, z_size)
    lists = lax.dynamic_slice_in_dim(block_lists[:, :, 1], my_y * GROUP, GROUP, axis=0)
    lists = lax.dynamic_index_in_dim(lists.reshape(mine), my_z, 2, keepdims=False)
    counts = lax.dynamic_slice_in_dim(block_counts, my_y * GROUP, GROUP, axis=0)
    counts = lax.dynamic_index_in_dim(counts.reshape(mine), my_z, 2, keepdims=False)
    other = lists % z_size * y_size + lists // z_size
    own = my_z * y_size + jnp.arange(y_size, dtype=jnp.int32)

    raised, wg, stats = own_part(kv_head, got)
    dkv_all, score_grads = key_part(other, counts, own, kv_all, got, raised, wg, stats)
    dkv_head = lax.psum_scatter(dkv_all, "z", scatter_dimension=0, tiled=True)

    dq_head, dbq_part = query_part(other, kv_all, kv_head, score_grads)
    dbq_z = jnp.sum(lax.all_gather(dbq_part, "z", axis=0), axis=0)
    dbq_rows = pieces(lax.all_gather(dbq_z, REP, axis=0))
    dbq_rows = jnp.broadcast_to(dbq_rows, (groups,) + dbq_rows.shape)
    back = exchange(jnp.concatenate([dq_head, dbq_rows], axis=1))
    dq_out = side_by_side(back[:, :BLOCK])[None]
    dbq_out = jnp.sum(back[:, BLOCK : BLOCK + 3].astype(jnp.float32), axis=1).reshape(-1)

    dk_out, dv_out = join_heads(exchange(dkv_head))
    dk_out, dv_out = dk_out[None], dv_out[None]
    return dq_out, dk_out, dv_out, dbq_out


def solution(mesh):
    torus = Mesh(mesh.devices.reshape(4, 16, 4, 2), ("y", "z", "x", "core"))
    split = P(REP, SEQ, None)
    return jax.shard_map(
        body,
        mesh=torus,
        in_specs=(split, split, split, split, P(), P(), P()),
        out_specs=(split, split, split, P()),
        check_vma=False,
    )
```

time: 212 us -> 210 us (level)
  waiting for transfers between devices: 102 us -> 73.1 us
  blocking collectives: 52.8 us -> 73.9 us
  local copies, waits for them, and re-layouts: 12.8 us -> 19.6 us
  starting transfers between devices: 12.2 us -> 8.56 us
  Pallas kernels: 14.3 us -> 17 us
    reduce_scatter x1, waiting for transfers between devices: 30.6 us -> 7.4 us  [body(): dkv_head = lax.psum_scatter(dkv_all, 'z', scatter_dimension=0, tiled=True)]
    all_to_all x0 -> x1, blocking collectives: none -> 21.1 us  [body(): back = exchange(jnp.concatenate([dq_head, dbq_rows], axis=1))]
    unnamed x19 -> x30, local copies, waits for them, and re-layouts: 8.28 us -> 15 us
    all_gather x1, waiting for transfers between devices: 43.8 us -> 39 us  [body(): kv_all = lax.all_gather(kv_head, 'z', axis=0, tiled=True)]
    all_to_all x2 -> x1, starting transfers between devices: 8.42 us -> 4.74 us  [body(): dk_out, dv_out = join_heads(exchange(dkv_head))]
    pallas_call x2 -> x4, Pallas kernels: 13.4 us -> 16.2 us  [the longest x1 12.6 us: key_part(): pl.pallas_call(key_kernel, grid_spec=pltpu.PrefetchScalarGridSpec(num_sca...]
    all_to_all x2 -> x1, waiting for transfers between devices: 4.97 us -> 3.97 us  [body(): dk_out, dv_out = join_heads(exchange(dkv_head))]
  transfers between devices with their start and end apart: 5 -> 4, of which waited for: 4 -> 4; matrix products, arithmetic and copies ran while one was open for 6% -> 6% of each run, Pallas kernels for 0% -> 2%
where the time goes in v4:
time: 210 us
  blocking collectives  73.9 us (35%)
  waiting for transfers between devices  73.1 us (35%)
  local copies, waits for them, and re-layouts  19.6 us (9%)
  Pallas kernels  17 us (8%)
  between operations  14.2 us (7%)
  starting transfers between devices  8.56 us (4%)
  other arithmetic  3.08 us (1%)
    all_gather x1, waiting for transfers between devices, body(): kv_all = lax.all_gather(kv_head, 'z', axis=0, tiled=True)  39 us
    all_gather x1, blocking collectives, body(): dbq_z = jnp.sum(lax.all_gather(dbq_part, 'z', axis=0), axis=0)  29 us
    all_to_all x1, waiting for transfers between devices, body(): got = exchange(qg)  22.7 us
    all_to_all x1, blocking collectives, body(): back = exchange(jnp.concatenate([dq_head, dbq_rows], axis=1))  21.1 us
    unnamed x30, local copies, waits for them, and re-layouts  15 us
    all_gather x1, blocking collectives, body(): dbq_rows = pieces(lax.all_gather(dbq_z, REP, axis=0))  12.8 us
    pallas_call x1, Pallas kernels, key_part(): pl.pallas_call(key_kernel, grid_spec=pltpu.PrefetchScalarGridSpec(num_sca...  12.6 us
    all_to_all x1, blocking collectives, body(): kv_head = exchange(split_heads(k_lin[0], value_projection[0], groups))  11 us
  transfers between devices with their start and end apart: 4, of which 4 were waited for; matrix products, arithmetic and copies ran while one was open for 6% of the time, Pallas kernels for 2%

profile of v4, /device:TPU:2, one launch (start us, length us, event | category | flops | bytes accessed | tf_op | source)
XLA Modules:
  0.0 209.5 jit_solution(8629052074033367522)
XLA Ops:
  7.2 0.0 copy-start
  7.2 0.0 all-gather.4.cloned.1.call-start
  7.2 0.9 copy-done.8
  8.1 0.9 copy-done.9
  9.1 11.0 %all_to_all.20.kv_ref.own_ref = bf16[4,2,128,128]{3,2,1,0:T(8,128)(2,1)} all-to-all(bf16[4,2,128,128]{3,2,1,0:T(8,128)(2,1)S(1)} %shard_map.102), channel_id=1, replica_groups=mesh['y'=4,'z'=16,'x'=4,'core'=2] {'y'}, dimensions={0} | all-to-all | bytes 524288 | tf_op jit(solution)/shard_map/all_to_all | solution.py:319
  20.1 0.0 all-gather.4.cloned.1.call-update
  20.2 0.7 add.44
  20.9 1.6 copy.35
  22.5 0.5 copy.36
  23.0 1.6 copy.37
  24.7 1.3 copy.38
  26.0 0.3 fusion
  26.3 1.0 copy-done.11
  27.2 1.5 pad_maximum_fusion
  28.8 3.7 %all-to-all-start.1 = ((bf16[4,2,128,1024]{3,2,1,0:T(8,128)(2,1)}), bf16[4,2,128,1024]{3,2,1,0:T(8,128)(2,1)S(1)}, u32[]{:S(2)}, u32[]{:S(2)}) async-start(bf16[4,2,128,1024]{3,2,1,0:T(8,128)(2,1)} %pad_maximum_fusion), calls=%async_computation.1 | async-start | bytes 4194304 | tf_op jit(solution)/shard_map/all_to_all | solution.py:324
  32.5 0.0 reduce-scatter.2.cloned.1.call-start
  32.6 0.1 reshape.30
  32.7 0.1 reshape.29
  32.8 0.1 constant_dynamic-slice_fusion
  32.9 0.1 copy.34
  33.0 0.7 copy.39.count_ref
  33.7 0.1 copy.29
  33.8 0.1 copy.30
  33.9 0.5 iota_add_fusion.own_ref
  34.4 0.6 fusion.2.other_ref
  35.0 22.7 %all-to-all-done.1.qg_ref = bf16[4,2,128,1024]{3,2,1,0:T(8,128)(2,1)S(1)} async-done(((bf16[4,2,128,1024]{3,2,1,0:T(8,128)(2,1)}), bf16[4,2,128,1024]{3,2,1,0:T(8,128)(2,1)S(1)}, u32[]{:S(2)}, u32[]{:S(2)}) %all-to-all-start.1) | async-done | bytes 2097184 | tf_op jit(solution)/shard_map/all_to_all | solution.py:324
  57.7 1.4 shard_map.103
  59.1 1.3 copy-done.5
  60.5 1.3 copy-done.6
  61.8 0.7 copy-done.7
  62.5 39.0 %all-gather.4.cloned.1.call-done.kv_hbm.kv_ref = bf16[64,2,128,128]{3,2,1,0:T(8,128)(2,1)} async-done(((bf16[4,2,128,128]{3,2,1,0:T(8,128)(2,1)}), bf16[64,2,128,128]{3,2,1,0:T(8,128)(2,1)}) %all-gather.4.cloned.1.call-update) | async-done | bytes 4194320 | tf_op jit(solution)/shard_map/all_gather | solution.py:320
  101.5 12.6 %shard_map.104 = (bf16[64,2,128,128]{3,2,1,0:T(8,128)(2,1)}, bf16[4,2,128,1024]{3,2,1,0:T(8,128)(2,1)}) custom-call(s32[8,4]{1,0:T(8,128)} %fusion.2.other_ref, s32[8,4]{1,0:T(8,128)} %copy.39.count_ref, s32[4]{0:T(128)} %iota_add_fusion.own_ref, bf16[64,2,128,128]{3,2,1,0:T(8,128)(2,1)} %all-gather.4.cloned.1.call-done.kv_hbm.kv_ref, ...), custom_call_target="tpu_custom_call" | custom-call | flops 805306368 | bytes 16777216 | tf_op jit(solution)/shard_map/pallas_call | solution.py:160
  114.2 0.0 reduce-scatter.2.cloned.1.call-update
  114.2 1.5 copy-done.4
  115.7 2.2 %copy-done.2 = bf16[64,2,128,128]{3,2,1,0:T(8,128)(2,1)S(1)} copy-done((bf16[64,2,128,128]{3,2,1,0:T(8,128)(2,1)S(1)}, bf16[64,2,128,128]{3,2,1,0:T(8,128)(2,1)}, u32[]{:S(2)}) %copy-start.2) | copy-done | bytes 4194328
  117.9 2.1 shard_map.105
  120.0 29.0 %all-gather = f32[128,128]{1,0:T(8,128)S(1)} all-gather(f32[8,128]{1,0:T(8,128)S(1)} %get-tuple-element.18), channel_id=2, replica_groups=mesh['y'=4,'z'=16,'x'=4,'core'=2] {'z'}, dimensions={0}, use_global_device_ids=true | all-gather | bytes 69632 | tf_op jit(solution)/shard_map/all_gather | solution.py:339
  149.0 12.8 %all-gather.1 = f32[64,128]{1,0:T(8,128)S(1)} all-gather(f32[8,128]{1,0:T(8,128)S(1)} %bitcast_reduce_fusion), channel_id=3, replica_groups=mesh['y'=4,'z'=16,'x'=4,'core'=2] {'x','core'}, dimensions={0}, use_global_device_ids=true | all-gather | bytes 36864 | tf_op jit(solution)/shard_map/all_gather | solution.py:340
  161.9 0.1 pad_maximum_fusion.1
  162.0 21.1 %all_to_all.21 = bf16[4,144,1024]{2,1,0:T(8,128)(2,1)S(1)} all-to-all(bf16[4,144,1024]{2,1,0:T(8,128)(2,1)S(1)} %pad_maximum_fusion.1), channel_id=1, replica_groups=mesh['y'=4,'z'=16,'x'=4,'core'=2] {'y'}, dimensions={0} | all-to-all | bytes 2359296 | tf_op jit(solution)/shard_map/all_to_all | solution.py:342
  183.0 7.4 %reduce-scatter.2.cloned.1.call-done = bf16[4,2,128,128]{3,2,1,0:T(8,128)(2,1)} async-done(((bf16[64,2,128,128]{3,2,1,0:T(8,128)(2,1)}), bf16[4,2,128,128]{3,2,1,0:T(8,128)(2,1)}) %reduce-scatter.2.cloned.1.call-update) | async-done | bytes 262160 | tf_op jit(solution)/shard_map/reduce_scatter | solution.py:336
  190.4 4.7 %all-to-all-start.3 = ((bf16[4,2,128,128]{3,2,1,0:T(8,128)(2,1)}), bf16[4,2,128,128]{3,2,1,0:T(8,128)(2,1)S(1)}, u32[]{:S(2)}, u32[]{:S(2)}) async-start(bf16[4,2,128,128]{3,2,1,0:T(8,128)(2,1)} %reduce-scatter.2.cloned.1.call-done), calls=%async_computation.4 | async-start | bytes 524288 | tf_op jit(solution)/shard_map/all_to_all | solution.py:346
  195.2 0.1 slice_bitcast_fusion
  195.3 0.7 copy.40
  195.9 1.3 copy.41
  197.3 0.6 copy.44
  197.9 4.0 %all-to-all-done.3.x_any = bf16[4,2,128,128]{3,2,1,0:T(8,128)(2,1)S(1)} async-done(((bf16[4,2,128,128]{3,2,1,0:T(8,128)(2,1)}), bf16[4,2,128,128]{3,2,1,0:T(8,128)(2,1)S(1)}, u32[]{:S(2)}, u32[]{:S(2)}) %all-to-all-start.3) | async-done | bytes 262176 | tf_op jit(solution)/shard_map/all_to_all | solution.py:346
  201.9 0.8 shard_map.107
  (25 shorter events, 0.2 us)
Async XLA Ops:
  7.2 25.4 %copy-start = (s32[32,64]{1,0:T(8,128)S(1)}, s32[32,64]{1,0:T(8,128)}, u32[]{:S(2)}) copy-start(s32[32,64]{1,0:T(8,128)} %param.13) | copy-start | bytes 24580
  7.2 94.3 %all-gather.4.cloned.1.call-start = ((), (), s32[]{:S(2)}) async-start(), calls=%async_computation.5 | async-start | bytes 4456448 | tf_op jit(solution)/shard_map/all_gather | solution.py:320
  7.2 0.9 copy-start.8
  8.1 0.9 copy-start.9
  26.0 1.2 copy-start.11
  28.7 3.9 %copy-start.12 = (s32[32,64,2]{1,2,0:T(2,128)S(1)}, s32[32,64,2]{1,2,0:T(2,128)}, u32[]{:S(2)}) copy-start(s32[32,64,2]{1,2,0:T(2,128)} %param.12) | copy-start | bytes 49156
  28.8 28.9 %copy-start.3 = (bf16[4,2,128,128]{3,2,1,0:T(8,128)(2,1)S(1)}, bf16[4,2,128,128]{3,2,1,0:T(8,128)(2,1)}, u32[]{:S(2)}) copy-start(bf16[4,2,128,128]{3,2,1,0:T(8,128)(2,1)} %all_to_all.20.kv_ref.own_ref) | copy-start | bytes 786436
  28.8 28.9 %all-to-all-start.1 = ((bf16[4,2,128,1024]{3,2,1,0:T(8,128)(2,1)}), bf16[4,2,128,1024]{3,2,1,0:T(8,128)(2,1)S(1)}, u32[]{:S(2)}, u32[]{:S(2)}) async-start(bf16[4,2,128,1024]{3,2,1,0:T(8,128)(2,1)} %pad_maximum_fusion), calls=%async_computation.1 | async-start | bytes 4194304 | tf_op jit(solution)/shard_map/all_to_all | solution.py:324
  32.5 158.0 %reduce-scatter.2.cloned.1.call-start = ((), (), s32[]{:S(2)}) async-start(), calls=%async_computation.6 | async-start | bytes 4456448 | tf_op jit(solution)/shard_map/reduce_scatter | solution.py:336
  57.7 43.8 %copy-start.1 = (bf16[4,2,128,1024]{3,2,1,0:T(8,128)(2,1)}, bf16[4,2,128,1024]{3,2,1,0:T(8,128)(2,1)S(1)}, u32[]{:S(2)}) copy-start(bf16[4,2,128,1024]{3,2,1,0:T(8,128)(2,1)S(1)} %all-to-all-done.1.qg_ref) | copy-start | bytes 6291460
  59.1 1.3 copy-start.5
  60.5 1.3 copy-start.6
  61.8 0.7 copy-start.7
  114.1 1.6 copy-start.4
  114.2 1.6 copy-start.10
  115.7 2.2 %copy-start.2 = (bf16[64,2,128,128]{3,2,1,0:T(8,128)(2,1)S(1)}, bf16[64,2,128,128]{3,2,1,0:T(8,128)(2,1)}, u32[]{:S(2)}) copy-start(bf16[64,2,128,128]{3,2,1,0:T(8,128)(2,1)} %all-gather.4.cloned.1.call-done.kv_hbm.kv_ref) | copy-start | bytes 12582916
  190.4 11.4 %all-to-all-start.3 = ((bf16[4,2,128,128]{3,2,1,0:T(8,128)(2,1)}), bf16[4,2,128,128]{3,2,1,0:T(8,128)(2,1)S(1)}, u32[]{:S(2)}, u32[]{:S(2)}) async-start(bf16[4,2,128,128]{3,2,1,0:T(8,128)(2,1)} %reduce-scatter.2.cloned.1.call-done), calls=%async_computation.4 | async-start | bytes 524288 | tf_op jit(solution)/shard_map/all_to_all | solution.py:346
Sparse Core Ops, SparseCore 0:
  20.3 81.1 all-gather.3
  114.3 76.0 reduce-scatter.1
